TPU v7x, 128 devices: a whole 4x4x4 slice. The times are simulated.
128 devices in a mesh: dp: 16 (over y, z), expert: 8 (over x, core).
Axes of the slice: x: 4, y: 4, z: 4, core: 2. Of those that a mesh axis runs over, the one named last changes fastest.
Arguments:
- tokens: bfloat16 [16384, 8192], P(('dp', 'expert')), may hold values from -6 to 6
- modality: int32 [16384], P(('dp', 'expert')), may hold values from 0 to 1, as said below
- norm_gain: float32 [2, 8192], replicated, may hold values from 0.1 to 1.9
- picks: int32 [8, 128, 8], P(None, ('dp', 'expert')), may hold values from 0 to 16383, as said below
- counts: int32 [8, 128], replicated, may hold values from 0 to 8, as said below
- router: bfloat16 [8, 8192], P('expert'), may hold values from -0.0625 to 0.0625
- gate_weight: bfloat16 [8, 8192, 4096], P('expert', None, 'dp'), may hold values from -0.0625 to 0.0625
- up_weight: bfloat16 [8, 8192, 4096], P('expert', None, 'dp'), may hold values from -0.0625 to 0.0625
- down_weight: bfloat16 [8, 4096, 8192], P('expert', 'dp'), may hold values from -0.09375 to 0.09375
Outputs:
- mixed: bfloat16 [16384, 8192], P(('dp', 'expert'))
Inputs may be any that keep to these rules, and one draw needn't show every extreme that they name: `modality`: each device's 128 tokens hold at least 8 text and 8 image tokens. picks[e, s, k] names a token of device s (rows s * 128 to (s + 1) * 128 - 1); the 8 entries of one list are distinct tokens whose modality is 0 for e < 4 and 1 otherwise; only the first counts[e, s] of them are chosen, the rest is padding. For each expert and each dp index j, the counts of the devices j * 8 to (j + 1) * 8 - 1 add up to at most 32; for every expert some dp index reaches 32.
All inputs are finite; a program needn't handle non-finite values.
Results may differ from a plain program's by a relative error of at most 0.0095.
Values may be sent and summed in bfloat16 or wider, within the bound.
A program may use at most 128 MiB of HBM per device.

v0:
```python
import jax
import jax.numpy as jnp
from jax import lax
from jax.sharding import PartitionSpec as P

EPSILON = 1e-05


def expert_block(chosen, router, gate_weight, up_weight, down_weight):
    piece = lax.all_gather(chosen, "dp", axis=0, tiled=True)
    gate_value = jnp.dot(piece, gate_weight[0], preferred_element_type=jnp.float32)
    up_value = jnp.dot(piece, up_weight[0], preferred_element_type=jnp.float32)
    hidden_hidden = (jax.nn.silu(gate_value) * up_value).astype(jnp.bfloat16)
    router_score = jnp.dot(piece, router[0], preferred_element_type=jnp.float32)
    weight = jax.nn.sigmoid(router_score)
    return lax.psum_scatter(
        (
            weight[:, None]
            * jnp.dot(hidden_hidden, down_weight[0], preferred_element_type=jnp.float32)
        ).astype(jnp.bfloat16),
        "dp",
        scatter_dimension=0,
        tiled=True,
    )


def shards(tokens, modality, norm_gain, picks, counts, router, gate_weight, up_weight, down_weight):
    tok_rows = tokens.shape[0]
    groups = lax.axis_size("expert")
    pick_slots = picks.shape[2]
    flat_index = lax.axis_index(("dp", "expert"))
    values = tokens.astype(jnp.float32)
    square = jnp.mean(values * values, axis=1, keepdims=True)
    gain_rows = jnp.where(modality[:, None] == 1, norm_gain[1][None, :], norm_gain[0][None, :])
    normed = (values * lax.rsqrt(square + EPSILON) * gain_rows).astype(jnp.bfloat16)
    local_rows = picks[:, 0, :] - flat_index * tok_rows
    outgoing = jnp.take(normed, local_rows.reshape(-1), axis=0).reshape(groups, pick_slots, -1)
    incoming = lax.all_to_all(outgoing, "expert", split_axis=0, concat_axis=0, tiled=True)
    chosen = incoming.reshape(groups * pick_slots, -1)
    answers = expert_block(chosen, router, gate_weight, up_weight, down_weight)
    returned = lax.all_to_all(
        answers.reshape(groups, pick_slots, -1), "expert", split_axis=0, concat_axis=0, tiled=True
    )
    own_counts = lax.dynamic_index_in_dim(counts, flat_index, 1, keepdims=False)
    usable = (jnp.arange(pick_slots)[None, :] < own_counts[:, None]).reshape(-1)
    placing = (
        (local_rows.reshape(-1)[None, :] == jnp.arange(tok_rows)[:, None]) & usable[None, :]
    ).astype(jnp.bfloat16)
    combined = jnp.dot(
        placing, returned.reshape(groups * pick_slots, -1), preferred_element_type=jnp.float32
    )
    return (values + combined).astype(jnp.bfloat16)


def solution(mesh):
    placed = (
        P(("dp", "expert"), None),
        P(("dp", "expert")),
        P(),
        P(None, ("dp", "expert"), None),
        P(),
        P("expert", None),
        P("expert", None, "dp"),
        P("expert", None, "dp"),
        P("expert", "dp", None),
    )
    return jax.shard_map(
        shards, mesh=mesh, in_specs=placed, out_specs=P(("dp", "expert"), None), check_vma=False
    )
```

profile of v0, /device:TPU:1, one launch (start us, length us, event | category | flops | bytes accessed | tf_op | source)
XLA Modules:
  0.0 319.9 jit_solution(16163961582600901727)
XLA Ops:
  6.5 0.0 copy-start
  6.5 0.0 all-gather.2.cloned.1.call-start
  6.5 0.7 compare_and_fusion
  7.2 0.1 sub.34
  7.3 1.0 fusion.23
  8.3 2.1 fusion.1
  10.4 0.7 broadcast_compare_fusion
  11.1 2.3 fusion.3
  13.4 1.2 gather_fusion
  14.6 0.2 bitcast_select_fusion
  14.7 20.8 %all_to_all.10 = bf16[8,8,8192]{2,1,0:T(8,128)(2,1)} all-to-all(bf16[8,8,8192]{2,1,0:T(8,128)(2,1)S(1)} %bitcast_select_fusion), channel_id=1, replica_groups=mesh['dp'=16,'expert'=8] {'expert'}, dimensions={0} | all-to-all | bytes 2097152 | tf_op jit(solution)/shard_map/all_to_all | solution.py:38
  35.5 0.0 all-gather.2.cloned.1.call-update
  35.5 0.2 reduce-scatter.2.cloned.1.call-start
  35.8 112.2 %all-gather.2.cloned.1.call-done = bf16[1024,8192]{1,0:T(8,128)(2,1)} async-done(((bf16[64,8192]{1,0:T(8,128)(2,1)}), bf16[1024,8192]{1,0:T(8,128)(2,1)}) %all-gather.2.cloned.1.call-update) | async-done | bytes 16777232 | tf_op jit(solution)/shard_map/all_gather | solution.py:10
  148.0 0.0 copy-done
  148.0 0.0 copy-start.2
  148.0 10.3 %fusion.18 = f32[1,1024]{1,0:T(1,128)S(1)} fusion(bf16[1024,8192]{1,0:T(8,128)(2,1)} %all-gather.2.cloned.1.call-done, bf16[1,8192]{1,0:T(2,128)(2,1)S(1)} %copy-done), kind=kOutput, calls=%fused_computation.20 | convolution fusion | flops 16777216 | bytes 16797696 | tf_op jit(solution)/shard_map/dot_general | solution.py:14
  158.4 0.2 copy-done.2
  158.6 0.0 copy-start.4
  158.6 6.9 %fusion.7 = f32[1024,256]{1,0:T(8,128)S(1)} fusion(bf16[1024,8192]{1,0:T(8,128)(2,1)S(1)} %copy-done.2, bf16[1,8192,256]{2,1,0:T(8,128)(2,1)} %param.15), kind=kOutput, calls=%fused_computation.12 | convolution fusion | flops 4294967296 | bytes 22020096 | tf_op jit(solution)/shard_map/dot_general | solution.py:11
  165.4 0.0 copy-done.4
  165.4 4.5 %fusion.12 = bf16[1024,256]{1,0:T(8,128)(2,1)S(1)} fusion(bf16[1024,8192]{1,0:T(8,128)(2,1)S(1)} %copy-done.2, bf16[1,8192,256]{2,1,0:T(8,128)(2,1)S(1)} %copy-done.4, f32[1024,256]{1,0:T(8,128)S(1)} %fusion.7), kind=kOutput, calls=%fused_computation.15 | convolution fusion | flops 4296540160 | bytes 22544384 | tf_op jit(solution)/shard_map/dot_general | solution.py:12
  170.0 10.6 %multiply_convert_fusion = bf16[1024,8192]{1,0:T(8,128)(2,1)} fusion(bf16[1024,256]{1,0:T(8,128)(2,1)S(1)} %fusion.12, f32[1024]{0:T(1024)S(1)} %add_divide_fusion, bf16[1,256,8192]{2,1,0:T(8,128)(2,1)} %param.17), kind=kOutput, calls=%fused_computation.1 | convolution fusion | flops 4311744512 | bytes 21499904 | tf_op jit(solution)/shard_map/dot_general | solution.py:19
  180.5 0.0 copy-start.3
  180.5 0.0 copy-start.1
  180.5 0.0 reduce-scatter.2.cloned.1.call-update
  180.5 110.2 %reduce-scatter.2.cloned.1.call-done = bf16[64,8192]{1,0:T(8,128)(2,1)} async-done(((bf16[1024,8192]{1,0:T(8,128)(2,1)}), bf16[64,8192]{1,0:T(8,128)(2,1)}) %reduce-scatter.2.cloned.1.call-update) | async-done | bytes 1048592 | tf_op jit(solution)/shard_map/reduce_scatter | solution.py:16
  290.8 5.2 %all-to-all-start.1 = ((bf16[8,8,8192]{2,1,0:T(8,128)(2,1)}), bf16[8,8,8192]{2,1,0:T(8,128)(2,1)S(1)}, u32[]{:S(2)}, u32[]{:S(2)}) async-start(bf16[8,8,8192]{2,1,0:T(8,128)(2,1)} %bitcast.42), calls=%async_computation.2 | async-start | bytes 2097152 | tf_op jit(solution)/shard_map/all_to_all | solution.py:41
  296.0 0.1 sub.32
  296.0 0.0 copy-done.3
  296.1 0.2 dynamic-slice_reduce_fusion
  296.2 0.1 iota_compare_fusion.1
  296.3 0.1 lt.53
  296.4 14.7 %all-to-all-done.1 = bf16[8,8,8192]{2,1,0:T(8,128)(2,1)S(1)} async-done(((bf16[8,8,8192]{2,1,0:T(8,128)(2,1)}), bf16[8,8,8192]{2,1,0:T(8,128)(2,1)S(1)}, u32[]{:S(2)}, u32[]{:S(2)}) %all-to-all-start.1) | async-done | bytes 1048608 | tf_op jit(solution)/shard_map/all_to_all | solution.py:41
  311.1 0.0 copy-done.1
  311.1 2.0 fusion
  (4 shorter events, 0.0 us)
Async XLA Ops:
  6.5 141.5 %copy-start = (bf16[1,8192]{1,0:T(2,128)(2,1)S(1)}, bf16[1,8192]{1,0:T(2,128)(2,1)}, u32[]{:S(2)}) copy-start(bf16[1,8192]{1,0:T(2,128)(2,1)} %param.14) | copy-start | bytes 49156
  6.5 141.5 %all-gather.2.cloned.1.call-start = ((), (), s32[]{:S(2)}) async-start(), calls=%async_computation.3 | async-start | bytes 17825792 | tf_op jit(solution)/shard_map/all_gather | solution.py:10
  35.5 255.2 %reduce-scatter.2.cloned.1.call-start = ((), (), s32[]{:S(2)}) async-start(), calls=%async_computation.4 | async-start | bytes 17825792 | tf_op jit(solution)/shard_map/reduce_scatter | solution.py:16
  148.0 10.5 %copy-start.2 = (bf16[1024,8192]{1,0:T(8,128)(2,1)S(1)}, bf16[1024,8192]{1,0:T(8,128)(2,1)}, u32[]{:S(2)}) copy-start(bf16[1024,8192]{1,0:T(8,128)(2,1)} %all-gather.2.cloned.1.call-done) | copy-start | bytes 50331652
  158.6 6.9 %copy-start.4 = (bf16[1,8192,256]{2,1,0:T(8,128)(2,1)S(1)}, bf16[1,8192,256]{2,1,0:T(8,128)(2,1)}, u32[]{:S(2)}) copy-start(bf16[1,8192,256]{2,1,0:T(8,128)(2,1)} %param.16) | copy-start | bytes 12582916
  180.5 115.5 %copy-start.3 = (s32[8,128]{1,0:T(8,128)S(1)}, s32[8,128]{1,0:T(8,128)}, u32[]{:S(2)}) copy-start(s32[8,128]{1,0:T(8,128)} %param.13) | copy-start | bytes 12292
  180.5 130.6 %copy-start.1 = (bf16[128,8192]{1,0:T(8,128)(2,1)S(1)}, bf16[128,8192]{1,0:T(8,128)(2,1)}, u32[]{:S(2)}) copy-start(bf16[128,8192]{1,0:T(8,128)(2,1)} %param.9) | copy-start | bytes 6291460
  290.8 20.3 %all-to-all-start.1 = ((bf16[8,8,8192]{2,1,0:T(8,128)(2,1)}), bf16[8,8,8192]{2,1,0:T(8,128)(2,1)S(1)}, u32[]{:S(2)}, u32[]{:S(2)}) async-start(bf16[8,8,8192]{2,1,0:T(8,128)(2,1)} %bitcast.42), calls=%async_computation.2 | async-start | bytes 2097152 | tf_op jit(solution)/shard_map/all_to_all | solution.py:41
Sparse Core Ops, SparseCore 0:
  35.7 112.3 all-gather.1
  180.7 110.0 reduce-scatter.1
where the time goes:
time: 320 us
  waiting for transfers between devices  237 us (74%)
  matrix products  34.3 us (11%)
  blocking collectives  20.8 us (6%)
  between operations  13.5 us (4%)
  other arithmetic  6 us (2%)
  starting transfers between devices  5.44 us (2%)
    all_gather x1, waiting for transfers between devices, expert_block(): piece = lax.all_gather(chosen, 'dp', axis=0, tiled=True)  112 us
    reduce_scatter x1, waiting for transfers between devices, expert_block(): lax.psum_scatter((weight[:, None] * jnp.dot(hidden_hidden, down_weight[0]...  110 us
    all_to_all x1, blocking collectives, shards(): lax.all_to_all(outgoing, 'expert', split_axis=0, concat_axis=0, tiled=True)  20.8 us
    all_to_all x1, waiting for transfers between devices, shards(): lax.all_to_all(answers.reshape(groups, pick_slots, -1), 'expert', split_a...  14.7 us
    dot_general x1, matrix products, expert_block(): jnp.dot(hidden_hidden, down_weight[0], preferred_element_type=jnp.float32)  10.6 us
    dot_general x1, matrix products, expert_block(): router_score = jnp.dot(piece, router[0], preferred_element_type=jnp.float32)  10.3 us
    dot_general x1, matrix products, expert_block(): jnp.dot(piece, gate_weight[0], preferred_element_type=jnp.float32)  6.85 us
  transfers between devices with their start and end apart: 3, of which 3 were waited for; matrix products, arithmetic and copies ran while one was open for 0% of the time, Pallas kernels for 0%

commit v1 on v0

--- a/solution.py
+++ b/solution.py
@@ -36,8 +36,16 @@
     local_rows = picks[:, 0, :] - flat_index * tok_rows
     outgoing = jnp.take(normed, local_rows.reshape(-1), axis=0).reshape(groups, pick_slots, -1)
     incoming = lax.all_to_all(outgoing, "expert", split_axis=0, concat_axis=0, tiled=True)
-    chosen = incoming.reshape(groups * pick_slots, -1)
+    slots = incoming.reshape(groups * pick_slots, -1)
+    expert = lax.axis_index("expert")
+    group_counts = lax.dynamic_slice(counts, (expert, lax.axis_index("dp") * groups), (1, groups))[0]
+    live = (jnp.arange(pick_slots)[None, :] < group_counts[:, None]).reshape(-1)
+    place = jnp.cumsum(live.astype(jnp.int32)) - 1
+    live_rows = groups * pick_slots // 2
+    packing = ((jnp.arange(live_rows)[:, None] == place[None, :]) & live[None, :]).astype(jnp.bfloat16)
+    chosen = jnp.dot(packing, slots, preferred_element_type=jnp.float32).astype(jnp.bfloat16)
     answers = expert_block(chosen, router, gate_weight, up_weight, down_weight)
+    answers = jnp.dot(packing.T, answers, preferred_element_type=jnp.float32).astype(jnp.bfloat16)
     returned = lax.all_to_all(
         answers.reshape(groups, pick_slots, -1), "expert", split_axis=0, concat_axis=0, tiled=True
     )

time: 320 us -> 254 us (0.79)
  waiting for transfers between devices: 237 us -> 184 us
  blocking collectives: 20.8 us -> 0 us
  starting transfers between devices: 5.44 us -> 12.2 us
    all_gather x1, waiting for transfers between devices: 112 us -> 71.5 us  [expert_block(): piece = lax.all_gather(chosen, 'dp', axis=0, tiled=True)]
    reduce_scatter x1, waiting for transfers between devices: 110 us -> 83.6 us  [expert_block(): lax.psum_scatter((weight[:, None] * jnp.dot(hidden_hidden, down_weight[0]...]
    all_to_all x1 -> x0, blocking collectives: 20.8 us -> none  [shards(): lax.all_to_all(outgoing, 'expert', split_axis=0, concat_axis=0, tiled=True)]
    all_to_all x0 -> x1, waiting for transfers between devices: none -> 14.6 us  [shards(): lax.all_to_all(outgoing, 'expert', split_axis=0, concat_axis=0, tiled=True)]
    dot_general x1, matrix products: 10.6 us -> 17.9 us  [expert_block(): jnp.dot(hidden_hidden, down_weight[0], preferred_element_type=jnp.float32)]
    all_to_all x0 -> x1, starting transfers between devices: none -> 5.8 us  [shards(): lax.all_to_all(outgoing, 'expert', split_axis=0, concat_axis=0, tiled=True)]
    dot_general x1, matrix products: 10.3 us -> 5.79 us  [expert_block(): router_score = jnp.dot(piece, router[0], preferred_element_type=jnp.float32)]
  transfers between devices with their start and end apart: 3 -> 4, of which waited for: 3 -> 4; matrix products, arithmetic and copies ran while one was open for 0% -> 0% of each run, Pallas kernels for 0% -> 0%
where the time goes in v1:
time: 254 us
  waiting for transfers between devices  184 us (72%)
  matrix products  33.8 us (13%)
  between operations  13.5 us (5%)
  starting transfers between devices  12.2 us (5%)
  other arithmetic  7.26 us (3%)
  local copies, waits for them, and re-layouts  2.87 us (1%)
    reduce_scatter x1, waiting for transfers between devices, expert_block(): lax.psum_scatter((weight[:, None] * jnp.dot(hidden_hidden, down_weight[0]...  83.6 us
    all_gather x1, waiting for transfers between devices, expert_block(): piece = lax.all_gather(chosen, 'dp', axis=0, tiled=True)  71.5 us
    dot_general x1, matrix products, expert_block(): jnp.dot(hidden_hidden, down_weight[0], preferred_element_type=jnp.float32)  17.9 us
    all_to_all x1, waiting for transfers between devices, shards(): lax.all_to_all(answers.reshape(groups, pick_slots, -1), 'expert', split_a...  14.7 us
    all_to_all x1, waiting for transfers between devices, shards(): lax.all_to_all(outgoing, 'expert', split_axis=0, concat_axis=0, tiled=True)  14.6 us
    all_to_all x1, starting transfers between devices, shards(): lax.all_to_all(answers.reshape(groups, pick_slots, -1), 'expert', split_a...  6.18 us
    all_to_all x1, starting transfers between devices, shards(): lax.all_to_all(outgoing, 'expert', split_axis=0, concat_axis=0, tiled=True)  5.8 us
    dot_general x1, matrix products, expert_block(): router_score = jnp.dot(piece, router[0], preferred_element_type=jnp.float32)  5.79 us
  transfers between devices with their start and end apart: 4, of which 4 were waited for; matrix products, arithmetic and copies ran while one was open for 0% of the time, Pallas kernels for 0%

profile of v1, /device:TPU:1, one launch (start us, length us, event | category | flops | bytes accessed | tf_op | source)
XLA Modules:
  0.0 254.0 jit_solution(18220412514542988038)
XLA Ops:
  6.5 0.0 copy-start
  6.5 0.7 broadcast_compare_fusion
  7.2 2.1 fusion.2
  9.3 0.7 compare_and_fusion
  10.0 0.1 sub.42
  10.1 1.0 fusion.37
  11.1 2.3 fusion.4
  13.4 1.2 gather_fusion
  14.6 0.0 copy-start.3
  14.6 1.1 bitcast_select_fusion
  15.7 5.8 %all-to-all-start = ((bf16[8,8,8192]{2,1,0:T(8,128)(2,1)}), bf16[8,8,8192]{2,1,0:T(8,128)(2,1)S(1)}, u32[]{:S(2)}, u32[]{:S(2)}) async-start(bf16[8,8,8192]{2,1,0:T(8,128)(2,1)} %bitcast_select_fusion), calls=%async_computation | async-start | bytes 2097152 | tf_op jit(solution)/shard_map/all_to_all | solution.py:38
  21.5 0.0 all-gather.2.cloned.1.call-start
  21.5 0.0 copy-done.3
  21.5 0.1 dynamic-slice_bitcast_fusion
  21.6 0.1 iota_compare_fusion.2
  21.7 0.1 lt.99
  21.8 0.1 reshape.159
  21.9 0.1 reduce-window.8
  22.0 0.1 add_reduce_fusion
  22.1 14.6 %all-to-all-done = bf16[8,8,8192]{2,1,0:T(8,128)(2,1)S(1)} async-done(((bf16[8,8,8192]{2,1,0:T(8,128)(2,1)}), bf16[8,8,8192]{2,1,0:T(8,128)(2,1)S(1)}, u32[]{:S(2)}, u32[]{:S(2)}) %all-to-all-start) | async-done | bytes 1048608 | tf_op jit(solution)/shard_map/all_to_all | solution.py:38
  36.6 1.1 convolution_convert_fusion.1
  37.7 0.0 all-gather.2.cloned.1.call-update
  37.7 0.2 reduce-scatter.2.cloned.1.call-start
  38.0 71.5 %all-gather.2.cloned.1.call-done = bf16[512,8192]{1,0:T(8,128)(2,1)} async-done(((bf16[32,8192]{1,0:T(8,128)(2,1)}), bf16[512,8192]{1,0:T(8,128)(2,1)}) %all-gather.2.cloned.1.call-update) | async-done | bytes 8388624 | tf_op jit(solution)/shard_map/all_gather | solution.py:10
  109.5 0.0 copy-done
  109.5 0.0 copy-start.1
  109.5 5.8 %fusion.23 = f32[1,512]{1,0:T(1,128)S(1)} fusion(bf16[512,8192]{1,0:T(8,128)(2,1)} %all-gather.2.cloned.1.call-done, bf16[1,8192]{1,0:T(2,128)(2,1)S(1)} %copy-done), kind=kOutput, calls=%fused_computation.25 | convolution fusion | flops 8388608 | bytes 8407040 | tf_op jit(solution)/shard_map/dot_general | solution.py:14
  115.3 0.0 copy-done.1
  115.3 4.5 %fusion.8 = f32[512,256]{1,0:T(8,128)S(1)} fusion(bf16[512,8192]{1,0:T(8,128)(2,1)S(1)} %copy-done.1, bf16[1,8192,256]{2,1,0:T(8,128)(2,1)} %param.15), kind=kOutput, calls=%fused_computation.15 | convolution fusion | flops 2147483648 | bytes 13107200 | tf_op jit(solution)/shard_map/dot_general | solution.py:11
  119.8 17.9 %multiply_convert_fusion = bf16[512,8192]{1,0:T(8,128)(2,1)} fusion(f32[512]{0:T(512)S(1)} %add_divide_fusion, bf16[1,256,8192]{2,1,0:T(8,128)(2,1)} %param.17, bf16[512,8192]{1,0:T(8,128)(2,1)} %all-gather.2.cloned.1.call-done, bf16[1,8192,256]{2,1,0:T(8,128)(2,1)} %param.16, f32[512,256]{1,0:T(8,128)S(1)} %fusion.8), kind=kOutput, calls=%fused_computation.1 | convolution fusion | flops 4304142336 | bytes 25692160 | tf_op jit(solution)/shard_map/dot_general | solution.py:19
  137.7 0.0 copy-start.2
  137.7 0.0 reduce-scatter.2.cloned.1.call-update
  137.8 83.6 %reduce-scatter.2.cloned.1.call-done = bf16[32,8192]{1,0:T(8,128)(2,1)} async-done(((bf16[512,8192]{1,0:T(8,128)(2,1)}), bf16[32,8192]{1,0:T(8,128)(2,1)}) %reduce-scatter.2.cloned.1.call-update) | async-done | bytes 524304 | tf_op jit(solution)/shard_map/reduce_scatter | solution.py:16
  221.3 2.5 fusion.1
  223.8 6.2 %all-to-all-start.1 = ((bf16[8,8,8192]{2,1,0:T(8,128)(2,1)}), bf16[8,8,8192]{2,1,0:T(8,128)(2,1)S(1)}, u32[]{:S(2)}, u32[]{:S(2)}) async-start(bf16[8,8,8192]{2,1,0:T(8,128)(2,1)} %fusion.1), calls=%async_computation.2 | async-start | bytes 2097152 | tf_op jit(solution)/shard_map/all_to_all | solution.py:49
  230.0 0.1 sub.38
  230.1 0.2 dynamic-slice_reduce_fusion
  230.3 0.1 iota_compare_fusion.3
  230.4 0.1 lt.92
  230.5 14.7 %all-to-all-done.1 = bf16[8,8,8192]{2,1,0:T(8,128)(2,1)S(1)} async-done(((bf16[8,8,8192]{2,1,0:T(8,128)(2,1)}), bf16[8,8,8192]{2,1,0:T(8,128)(2,1)S(1)}, u32[]{:S(2)}, u32[]{:S(2)}) %all-to-all-start.1) | async-done | bytes 1048608 | tf_op jit(solution)/shard_map/all_to_all | solution.py:49
  245.1 0.0 copy-done.2
  245.1 2.0 fusion
  (4 shorter events, 0.0 us)
Async XLA Ops:
  6.5 103.0 %copy-start = (bf16[1,8192]{1,0:T(2,128)(2,1)S(1)}, bf16[1,8192]{1,0:T(2,128)(2,1)}, u32[]{:S(2)}) copy-start(bf16[1,8192]{1,0:T(2,128)(2,1)} %param.14) | copy-start | bytes 49156
  14.6 7.0 %copy-start.3 = (s32[8,128]{1,0:T(8,128)S(1)}, s32[8,128]{1,0:T(8,128)}, u32[]{:S(2)}) copy-start(s32[8,128]{1,0:T(8,128)} %param.13) | copy-start | bytes 12292
  15.7 20.9 %all-to-all-start = ((bf16[8,8,8192]{2,1,0:T(8,128)(2,1)}), bf16[8,8,8192]{2,1,0:T(8,128)(2,1)S(1)}, u32[]{:S(2)}, u32[]{:S(2)}) async-start(bf16[8,8,8192]{2,1,0:T(8,128)(2,1)} %bitcast_select_fusion), calls=%async_computation | async-start | bytes 2097152 | tf_op jit(solution)/shard_map/all_to_all | solution.py:38
  21.5 88.0 %all-gather.2.cloned.1.call-start = ((), (), s32[]{:S(2)}) async-start(), calls=%async_computation.3 | async-start | bytes 8912896 | tf_op jit(solution)/shard_map/all_gather | solution.py:10
  37.7 183.6 %reduce-scatter.2.cloned.1.call-start = ((), (), s32[]{:S(2)}) async-start(), calls=%async_computation.4 | async-start | bytes 8912896 | tf_op jit(solution)/shard_map/reduce_scatter | solution.py:16
  109.5 5.8 %copy-start.1 = (bf16[512,8192]{1,0:T(8,128)(2,1)S(1)}, bf16[512,8192]{1,0:T(8,128)(2,1)}, u32[]{:S(2)}) copy-start(bf16[512,8192]{1,0:T(8,128)(2,1)} %all-gather.2.cloned.1.call-done) | copy-start | bytes 25165828
  137.7 107.4 %copy-start.2 = (bf16[128,8192]{1,0:T(8,128)(2,1)S(1)}, bf16[128,8192]{1,0:T(8,128)(2,1)}, u32[]{:S(2)}) copy-start(bf16[128,8192]{1,0:T(8,128)(2,1)} %param.9) | copy-start | bytes 6291460
  223.8 21.3 %all-to-all-start.1 = ((bf16[8,8,8192]{2,1,0:T(8,128)(2,1)}), bf16[8,8,8192]{2,1,0:T(8,128)(2,1)S(1)}, u32[]{:S(2)}, u32[]{:S(2)}) async-start(bf16[8,8,8192]{2,1,0:T(8,128)(2,1)} %fusion.1), calls=%async_computation.2 | async-start | bytes 2097152 | tf_op jit(solution)/shard_map/all_to_all | solution.py:49
Sparse Core Ops, SparseCore 0:
  37.9 71.5 all-gather.1
  137.9 83.4 reduce-scatter.1

commit v2 on v0

v2 whole, which is shorter than its diff:
```python
import functools

import jax
import jax.numpy as jnp
from jax import lax
from jax.experimental import pallas as pl
from jax.experimental.pallas import tpu as pltpu
from jax.sharding import PartitionSpec as P

EPSILON = 1e-05
MESH = pl.DeviceIdType.MESH
SIDE = 4
GROUP = 8
CHUNKS = 4
F32 = jnp.float32
BF16 = jnp.bfloat16


def iota(shape, dim):
    return lax.broadcasted_iota(jnp.int32, shape, dim)


def kernel(
    tokens, gain, picks, counts, router, gate, up, down, out,
    tok, w1, w2, so, sr, x, acc, hid, part, r1, f1, red, r2, f2, ro, rr, ob, score, mats,
    local_sem, a2a_send, a2a_recv, ag_send, ag_p1, ag_p2, rs_send, rs_p1, rs_p2, ret_send, ret_recv, out_sem,
):
    dp, e = lax.axis_index("dp"), lax.axis_index("expert")
    y, z = dp // SIDE, dp % SIDE
    half = tokens.shape[1] // 2
    cols = half // CHUNKS
    ntok = tokens.shape[0]
    rows = x.shape[2] // (SIDE * SIDE)
    hr = rows // 2
    live_cap = rows

    def near(h, axis, step):
        along_y = (h == 0) == (axis == "a")
        if along_y:
            return (lax.rem(y + step + SIDE, SIDE) * SIDE + z, e)
        return (y * SIDE + lax.rem(z + step + SIDE, SIDE), e)

    def other(o):
        return (dp, lax.rem(e + o, GROUP))

    def send(src, dst, ssem, rsem, device):
        pltpu.make_async_remote_copy(
            src_ref=src, dst_ref=dst, send_sem=ssem, recv_sem=rsem, device_id=device, device_id_type=MESH
        ).start()

    def settle(ref, sem):
        pltpu.make_async_copy(ref, ref, sem).wait()

    barrier = pltpu.get_barrier_semaphore()
    for step in (-1, 1):
        for axis in "ab":
            pl.semaphore_signal(barrier, 1, device_id=near(0, axis, step), device_id_type=MESH)
    for o in range(1, GROUP):
        pl.semaphore_signal(barrier, 1, device_id=other(o), device_id_type=MESH)

    loads = []
    for h in range(2):
        cp = pltpu.make_async_copy(tokens.at[:, pl.ds(h * half, half)], tok.at[h], local_sem.at[h])
        cp.start()
        loads.append(cp)
    big = [
        pltpu.make_async_copy(gate.at[0], w1.at[:, pl.ds(0, gate.shape[2])], local_sem.at[2]),
        pltpu.make_async_copy(up.at[0], w1.at[:, pl.ds(gate.shape[2], gate.shape[2])], local_sem.at[3]),
        pltpu.make_async_copy(down.at[0], w2, local_sem.at[4]),
    ]

    nslot = GROUP * 16
    lane = iota((8, nslot), 1)
    lane_e, lane_h, lane_k = lane >> 4, (lane >> 3) & 1, lane & 7
    sub = iota((8, nslot), 0)
    pk = picks[:, 0, :] - (dp * GROUP + e) * ntok
    spread = jnp.zeros((8, nslot), jnp.int32)
    for k in range(8):
        spread = spread + jnp.where(lane_k == k, pk[:, k : k + 1], 0)
    pick_row = jnp.sum(jnp.where(sub == lane_e, spread, 0).astype(F32), axis=0, keepdims=True)
    cnt = jnp.sum(jnp.where(sub == e, counts[...], 0).astype(F32), axis=0, keepdims=True)
    cnt16 = jnp.broadcast_to(cnt, (16, nslot)).astype(BF16)
    src = iota((nslot, nslot), 0) - dp * GROUP
    dst_e = iota((nslot, nslot), 1) >> 4
    same = (src == dst_e).astype(F32).astype(BF16)
    before = ((src >= 0) & (src < dst_e)).astype(F32).astype(BF16)
    cnt_r = jnp.dot(cnt16, same, preferred_element_type=F32)[0:1]
    off_r = jnp.dot(cnt16, before, preferred_element_type=F32)[0:1]
    k_r = lane_k[0:1].astype(F32)
    pos_r = jnp.where(k_r < cnt_r, off_r + k_r, -1.0)

    def placing(n, shift):
        q = iota((2 * n, nslot), 0)
        l = iota((2 * n, nslot), 1)
        return ((q >> shift) == ((l >> 3) & 1)), (q & (n - 1)).astype(F32)

    same_half, t_id = placing(ntok, 7)
    put = jnp.where(same_half & (t_id == pick_row), 1.0, 0.0)
    same_half, p_id = placing(live_cap, 5)
    pack = jnp.where(same_half & (p_id == pos_r), 1.0, 0.0)
    take_m = put.T.astype(BF16)
    mats[0 : 2 * ntok, :] = put.astype(BF16)
    mats[2 * ntok : 2 * ntok + 2 * live_cap, :] = pack.astype(BF16)
    unpack_m = pack.T.astype(BF16)

    for cp in loads:
        cp.wait()
    for cp in big:
        cp.start()
    total = jnp.zeros((nslot, 128), F32)
    for k in range(CHUNKS):
        t = tok[:, :, pl.ds(k * cols, cols)].reshape(2 * ntok, cols)
        g = jnp.dot(take_m, t, preferred_element_type=F32)
        so[k] = g.astype(BF16).reshape(GROUP, 16, cols)
        sq = g * g
        for i in range(cols // 128):
            total = total + sq[:, i * 128 : (i + 1) * 128]
    ss = jnp.broadcast_to(jnp.sum(total, axis=1, keepdims=True), (nslot, 128))
    h_col = (iota((nslot, 128), 0) >> 3) & 1
    pair = jnp.where(h_col == 0, pltpu.roll(ss, nslot - 8, 0), pltpu.roll(ss, 8, 0))
    inv = lax.rsqrt((ss + pair)[:, 0:1] / (2 * half) + EPSILON)
    first = h_col[:, 0:1] == 0
    text = iota((nslot, 1), 0) < nslot // 2

    for k in range(CHUNKS):
        ga = gain[:, pl.ds(k * cols, cols)]
        gb = gain[:, pl.ds(half + k * cols, cols)]
        gm = jnp.where(
            first,
            jnp.where(text, ga[0:1], ga[1:2]),
            jnp.where(text, gb[0:1], gb[1:2]),
        )
        g = so[k].reshape(nslot, cols).astype(F32)
        so[k] = (g * inv * gm).astype(BF16).reshape(GROUP, 16, cols)
        if k == 0:
            pl.semaphore_wait(barrier, 4 + GROUP - 1)
        for o in (4, 3, 5, 2, 6, 7, 1):
            to = lax.rem(e + o, GROUP)
            send(so.at[k, to], sr.at[k, e], a2a_send.at[k], a2a_recv.at[k], other(o))
        sr[k, e] = so[k, e]

    score[...] = jnp.zeros_like(score)
    acc[...] = jnp.zeros_like(acc)

    def place(h, da, db):
        dy, dz = (da, db) if h == 0 else (db, da)
        return (dy * SIDE + dz) * rows

    def blk(h, k, da, db, part_=None):
        base = place(h, da, db)
        if part_ is None:
            return x.at[h, k, pl.ds(base, rows)]
        return x.at[h, k, pl.ds(base + part_ * hr, hr)]

    def second(h, k, da):
        s = ag_send.at[h, k]
        send(blk(h, k, da, 0), blk(h, k, da, 1), s, ag_p2.at[h, k, da, 0], near(h, "b", 1))
        send(blk(h, k, da, 0), blk(h, k, da, 3), s, ag_p2.at[h, k, da, 1], near(h, "b", -1))

    def stage_a(k):
        settle(sr.at[k, pl.ds(0, GROUP - 1)], a2a_recv.at[k])
        packed = jnp.dot(
            mats[2 * ntok : 2 * ntok + 2 * live_cap, :], sr[k].reshape(nslot, cols), preferred_element_type=F32
        )
        both = packed.astype(BF16)
        x[0, k, 0:rows] = both[0:rows]
        x[1, k, 0:rows] = both[rows : 2 * rows]
        for h in range(2):
            s = ag_send.at[h, k]
            send(blk(h, k, 0, 0), blk(h, k, 1, 0), s, ag_p1.at[h, k, 0], near(h, "a", 1))
            send(blk(h, k, 0, 0), blk(h, k, 3, 0), s, ag_p1.at[h, k, 1], near(h, "a", -1))
        for h in range(2):
            second(h, k, 0)
        prod = packed[0:rows] * router[:, pl.ds(k * cols, cols)].astype(F32)
        prod += packed[rows : 2 * rows] * router[:, pl.ds(half + k * cols, cols)].astype(F32)
        s = score[...]
        for i in range(cols // 128):
            s = s + prod[:, i * 128 : (i + 1) * 128]
        score[...] = s

    def stage_b(k):
        for h in range(2):
            s = ag_send.at[h, k]
            settle(blk(h, k, 1, 0), ag_p1.at[h, k, 0])
            send(blk(h, k, 1, 0, 0), blk(h, k, 2, 0, 0), s, ag_p1.at[h, k, 2], near(h, "a", 1))
            settle(blk(h, k, 3, 0), ag_p1.at[h, k, 1])
            send(blk(h, k, 3, 0, 1), blk(h, k, 2, 0, 1), s, ag_p1.at[h, k, 3], near(h, "a", -1))
        for h in range(2):
            second(h, k, 1)
            second(h, k, 3)

    def stage_c(k):
        for h in range(2):
            settle(blk(h, k, 2, 0, 0), ag_p1.at[h, k, 2])
            settle(blk(h, k, 2, 0, 1), ag_p1.at[h, k, 3])
            second(h, k, 2)

    def stage_d(k, das):
        for da in das:
            for h in range(2):
                s = ag_send.at[h, k]
                settle(blk(h, k, da, 1), ag_p2.at[h, k, da, 0])
                send(blk(h, k, da, 1, 0), blk(h, k, da, 2, 0), s, ag_p2.at[h, k, da, 2], near(h, "b", 1))
                settle(blk(h, k, da, 3), ag_p2.at[h, k, da, 1])
                send(blk(h, k, da, 3, 1), blk(h, k, da, 2, 1), s, ag_p2.at[h, k, da, 3], near(h, "b", -1))

    def stage_e(k):
        if k == 0:
            big[0].wait()
            big[1].wait()
        for h in range(2):
            for da in range(SIDE):
                settle(blk(h, k, da, 2, 0), ag_p2.at[h, k, da, 2])
                settle(blk(h, k, da, 2, 1), ag_p2.at[h, k, da, 3])
        for h in range(2):
            acc[...] += jnp.dot(x[h, k], w1[pl.ds(h * half + k * cols, cols), :], preferred_element_type=F32)

    stage_a(0)
    for k in range(CHUNKS):
        stage_b(k)
        stage_d(k, (0,))
        if k + 1 < CHUNKS:
            stage_a(k + 1)
        stage_c(k)
        stage_d(k, (1, 3))
        if k > 0:
            stage_e(k - 1)
        stage_d(k, (2,))
    stage_e(CHUNKS - 1)

    width = acc.shape[1] // 2
    gv, uv = acc[:, 0:width], acc[:, width : 2 * width]
    hid[...] = (gv / (1.0 + jnp.exp(-gv)) * uv).astype(BF16)
    weight = jax.nn.sigmoid(jnp.sum(score[...], axis=1, keepdims=True))
    big[2].wait()

    def multiply(k):
        for h in range(2):
            for t in range(0, cols, 256):
                w = w2[:, pl.ds(h * half + k * cols + t, 256)]
                v = jnp.dot(hid[...], w, preferred_element_type=F32).astype(BF16)
                for da in range(SIDE):
                    for db in range(SIDE):
                        base = place(h, da, db)
                        for q in range(2):
                            part[h, k, db, q, da * hr : (da + 1) * hr, t : t + 256] = v[
                                base + q * hr : base + (q + 1) * hr
                            ]
            s = rs_send.at[h, k, 0]
            send(part.at[h, k, 2, 0], r1.at[h, k, 0], s, rs_p1.at[h, k, 0], near(h, "b", -1))
            send(part.at[h, k, 2, 1], r1.at[h, k, 1], s, rs_p1.at[h, k, 1], near(h, "b", 1))
            send(part.at[h, k, 1, 1], f1.at[h, k, 0, 1], s, rs_p1.at[h, k, 2], near(h, "b", -1))
            send(part.at[h, k, 3, 0], f1.at[h, k, 1, 0], s, rs_p1.at[h, k, 3], near(h, "b", 1))

    def first_on(k):
        for h in range(2):
            s = rs_send.at[h, k, 0]
            settle(r1.at[h, k, 0], rs_p1.at[h, k, 0])
            part[h, k, 1, 0] = (part[h, k, 1, 0].astype(F32) + r1[h, k, 0].astype(F32)).astype(BF16)
            send(part.at[h, k, 1, 0], f1.at[h, k, 0, 0], s, rs_p1.at[h, k, 4], near(h, "b", -1))
            settle(r1.at[h, k, 1], rs_p1.at[h, k, 1])
            part[h, k, 3, 1] = (part[h, k, 3, 1].astype(F32) + r1[h, k, 1].astype(F32)).astype(BF16)
            send(part.at[h, k, 3, 1], f1.at[h, k, 1, 1], s, rs_p1.at[h, k, 5], near(h, "b", 1))

    def first_end(k):
        for h in range(2):
            settle(f1.at[h, k, 0, 1], rs_p1.at[h, k, 2])
            settle(f1.at[h, k, 1, 0], rs_p1.at[h, k, 3])
            settle(f1.at[h, k, 0, 0], rs_p1.at[h, k, 4])
            settle(f1.at[h, k, 1, 1], rs_p1.at[h, k, 5])
            for q in range(2):
                v = part[h, k, 0, q].astype(F32) + f1[h, k, 0, q].astype(F32) + f1[h, k, 1, q].astype(F32)
                v = v.astype(BF16)
                for da in range(SIDE):
                    red[h, k, da, q] = v[da * hr : (da + 1) * hr]
            s = rs_send.at[h, k, 1]
            send(red.at[h, k, 2, 0], r2.at[h, k, 0], s, rs_p2.at[h, k, 0], near(h, "a", -1))
            send(red.at[h, k, 2, 1], r2.at[h, k, 1], s, rs_p2.at[h, k, 1], near(h, "a", 1))
            send(red.at[h, k, 1, 1], f2.at[h, k, 0, 1], s, rs_p2.at[h, k, 2], near(h, "a", -1))
            send(red.at[h, k, 3, 0], f2.at[h, k, 1, 0], s, rs_p2.at[h, k, 3], near(h, "a", 1))

    def second_on(k):
        for h in range(2):
            s = rs_send.at[h, k, 1]
            settle(r2.at[h, k, 0], rs_p2.at[h, k, 0])
            red[h, k, 1, 0] = (red[h, k, 1, 0].astype(F32) + r2[h, k, 0].astype(F32)).astype(BF16)
            send(red.at[h, k, 1, 0], f2.at[h, k, 0, 0], s, rs_p2.at[h, k, 4], near(h, "a", -1))
            settle(r2.at[h, k, 1], rs_p2.at[h, k, 1])
            red[h, k, 3, 1] = (red[h, k, 3, 1].astype(F32) + r2[h, k, 1].astype(F32)).astype(BF16)
            send(red.at[h, k, 3, 1], f2.at[h, k, 1, 1], s, rs_p2.at[h, k, 5], near(h, "a", 1))

    def second_end(k):
        res = []
        for h in range(2):
            settle(f2.at[h, k, 0, 1], rs_p2.at[h, k, 2])
            settle(f2.at[h, k, 1, 0], rs_p2.at[h, k, 3])
            settle(f2.at[h, k, 0, 0], rs_p2.at[h, k, 4])
            settle(f2.at[h, k, 1, 1], rs_p2.at[h, k, 5])
            v = red[h, k, 0].astype(F32) + f2[h, k, 0].astype(F32) + f2[h, k, 1].astype(F32)
            res.append((v.reshape(rows, cols) * weight).astype(BF16))
        res = jnp.concatenate(res, axis=0)
        back = jnp.dot(unpack_m, res, preferred_element_type=F32)
        ro[k] = back.astype(BF16).reshape(GROUP, 16, cols)
        for o in (4, 3, 5, 2, 6, 7, 1):
            to = lax.rem(e + o, GROUP)
            send(ro.at[k, to], rr.at[k, e], ret_send.at[k], ret_recv.at[k], other(o))
        rr[k, e] = ro[k, e]

    def finish(k):
        settle(rr.at[k, pl.ds(0, GROUP - 1)], ret_recv.at[k])
        v = jnp.dot(mats[0 : 2 * ntok, :], rr[k].reshape(nslot, cols), preferred_element_type=F32)
        t = tok[:, :, pl.ds(k * cols, cols)].reshape(2 * ntok, cols).astype(F32)
        ob[k] = (t + v).astype(BF16).reshape(2, ntok, cols)
        for h in range(2):
            pltpu.make_async_copy(
                ob.at[k, h], out.at[:, pl.ds(h * half + k * cols, cols)], out_sem.at[h, k]
            ).start()

    multiply(0)
    for k in range(CHUNKS + 2):
        if k < CHUNKS:
            if k + 1 < CHUNKS:
                multiply(k + 1)
            first_on(k)
        if 0 <= k - 1 < CHUNKS:
            second_on(k - 1)
        if k < CHUNKS:
            first_end(k)
        if 0 <= k - 1 < CHUNKS:
            second_end(k - 1)
        if 0 <= k - 2 < CHUNKS:
            finish(k - 2)

    for k in range(CHUNKS):
        for h in range(2):
            settle(x.at[h, k, pl.ds(0, 15 * rows)], ag_send.at[h, k])
            settle(part.at[h, k, pl.ds(0, 3)], rs_send.at[h, k, 0])
            settle(red.at[h, k, pl.ds(0, 3)], rs_send.at[h, k, 1])
            pltpu.make_async_copy(
                ob.at[k, h], out.at[:, pl.ds(h * half + k * cols, cols)], out_sem.at[h, k]
            ).wait()
        settle(so.at[k, pl.ds(0, GROUP - 1)], a2a_send.at[k])
        settle(ro.at[k, pl.ds(0, GROUP - 1)], ret_send.at[k])


def shards(tokens, modality, norm_gain, picks, counts, router, gate_weight, up_weight, down_weight):
    ntok, d = tokens.shape
    half = d // 2
    cols = half // CHUNKS
    hidden = gate_weight.shape[2]
    rows = GROUP * picks.shape[2] // 2
    hr = rows // 2
    places = SIDE * SIDE
    vmem = pl.BlockSpec(memory_space=pltpu.VMEM)
    anywhere = pl.BlockSpec(memory_space=pl.ANY)
    dma = pltpu.SemaphoreType.DMA
    slots = rows * places
    flops = 2 * slots * d * hidden * 3
    return pl.pallas_call(
        kernel,
        name="expert_layer",
        out_shape=jax.ShapeDtypeStruct((ntok, d), BF16),
        in_specs=[anywhere, vmem, vmem, vmem, vmem, anywhere, anywhere, anywhere],
        out_specs=anywhere,
        scratch_shapes=[
            pltpu.VMEM((2, ntok, half), BF16),
            pltpu.VMEM((d, 2 * hidden), BF16),
            pltpu.VMEM((hidden, d), BF16),
            pltpu.VMEM((CHUNKS, GROUP, 16, cols), BF16),
            pltpu.VMEM((CHUNKS, GROUP, 16, cols), BF16),
            pltpu.VMEM((2, CHUNKS, slots, cols), BF16),
            pltpu.VMEM((slots, 2 * hidden), F32),
            pltpu.VMEM((slots, hidden), BF16),
            pltpu.VMEM((2, CHUNKS, SIDE, 2, SIDE * hr, cols), BF16),
            pltpu.VMEM((2, CHUNKS, 2, SIDE * hr, cols), BF16),
            pltpu.VMEM((2, CHUNKS, 2, 2, SIDE * hr, cols), BF16),
            pltpu.VMEM((2, CHUNKS, SIDE, 2, hr, cols), BF16),
            pltpu.VMEM((2, CHUNKS, 2, hr, cols), BF16),
            pltpu.VMEM((2, CHUNKS, 2, 2, hr, cols), BF16),
            pltpu.VMEM((CHUNKS, GROUP, 16, cols), BF16),
            pltpu.VMEM((CHUNKS, GROUP, 16, cols), BF16),
            pltpu.VMEM((CHUNKS, 2, ntok, cols), BF16),
            pltpu.VMEM((rows, 128), F32),
            pltpu.VMEM((2 * ntok + 2 * rows, GROUP * 16), BF16),
            dma((5,)),
            dma((CHUNKS,)),
            dma((CHUNKS,)),
            dma((2, CHUNKS)),
            dma((2, CHUNKS, 4)),
            dma((2, CHUNKS, SIDE, 4)),
            dma((2, CHUNKS, 2)),
            dma((2, CHUNKS, 6)),
            dma((2, CHUNKS, 6)),
            dma((CHUNKS,)),
            dma((CHUNKS,)),
            dma((2, CHUNKS)),
        ],
        compiler_params=pltpu.CompilerParams(
            collective_id=0, has_side_effects=True, vmem_limit_bytes=60 * 2**20
        ),
        cost_estimate=pl.CostEstimate(flops=flops, bytes_accessed=16 * 2**20, transcendentals=slots * hidden),
    )(tokens, norm_gain, picks, counts, router, gate_weight, up_weight, down_weight)


def solution(mesh):
    placed = (
        P(("dp", "expert"), None),
        P(("dp", "expert")),
        P(),
        P(None, ("dp", "expert"), None),
        P(),
        P("expert", None),
        P("expert", None, "dp"),
        P("expert", None, "dp"),
        P("expert", "dp", None),
    )
    return jax.shard_map(
        shards, mesh=mesh, in_specs=placed, out_specs=P(("dp", "expert"), None), check_vma=False
    )
```

time: 320 us -> 130 us (0.41)
  waiting for transfers between devices: 237 us -> 0 us
  Pallas kernels: 0 us -> 126 us
  matrix products: 34.3 us -> 0 us
  blocking collectives: 20.8 us -> 0 us
  between operations: 13.5 us -> 0.01 us
  other arithmetic: 6 us -> 0 us
  starting transfers between devices: 5.44 us -> 0 us
    pallas_call x0 -> x1, Pallas kernels: none -> 126 us  [shards(): pl.pallas_call(kernel, name='expert_layer', out_shape=jax.ShapeDtypeStruc...]
    all_gather x1 -> x0, waiting for transfers between devices: 112 us -> none  [expert_block(): piece = lax.all_gather(chosen, 'dp', axis=0, tiled=True)]
    reduce_scatter x1 -> x0, waiting for transfers between devices: 110 us -> none  [expert_block(): lax.psum_scatter((weight[:, None] * jnp.dot(hidden_hidden, down_weight[0]...]
    dot_general x5 -> x0, matrix products: 34.3 us -> none  [the longest x1 10.6 us: expert_block(): jnp.dot(hidden_hidden, down_weight[0], preferred_element_type=jnp.float32)]
    all_to_all x1 -> x0, blocking collectives: 20.8 us -> none  [shards(): lax.all_to_all(outgoing, 'expert', split_axis=0, concat_axis=0, tiled=True)]
    all_to_all x1 -> x0, waiting for transfers between devices: 14.7 us -> none  [shards(): lax.all_to_all(answers.reshape(groups, pick_slots, -1), 'expert', split_a...]
    all_to_all x1 -> x0, starting transfers between devices: 5.21 us -> none  [shards(): lax.all_to_all(answers.reshape(groups, pick_slots, -1), 'expert', split_a...]
  transfers between devices with their start and end apart: 3 -> 0, of which waited for: 3 -> 0; matrix products, arithmetic and copies ran while one was open for 0% -> 0% of each run, Pallas kernels for 0% -> 0%
where the time goes in v2:
time: 130 us; the launch traced here: 129 us
  Pallas kernels  126 us (97%)
  local copies, waits for them, and re-layouts  3.1 us (2%)
    pallas_call x1, Pallas kernels, shards(): pl.pallas_call(kernel, name='expert_layer', out_shape=jax.ShapeDtypeStruc...  126 us
    unnamed x1, local copies, waits for them, and re-layouts  3.1 us

profile of v2, /device:TPU:1, one launch (start us, length us, event | category | flops | bytes accessed | tf_op | source)
XLA Modules:
  0.0 129.5 jit_solution(16203548729941946171)
XLA Ops:
  0.0 126.4 %expert_layer.1 = bf16[128,8192]{1,0:T(8,128)(2,1)} custom-call(bf16[128,8192]{1,0:T(8,128)(2,1)} %tokens.1, f32[2,8192]{1,0:T(2,128)} %gain.1, s32[8,1,8]{2,1,0:T(1,128)} %picks.1, s32[8,128]{1,0:T(8,128)} %counts.1, bf16[1,8192]{1,0:T(2,128)(2,1)} %router.1, bf16[1,8192,256]{2,1,0:T(8,128)(2,1)} %gate.1, bf16[1,8192,256]{2,1,0:T(8,128)(2,1)} %up.1, ...), custom_call_target="tpu_custom_call" | custom-call | flops 6442450944 | bytes 16777216 | tf_op jit(solution)/shard_map/expert_layer/pallas_call | solution.py:359
  126.4 3.1 %copy.10 = bf16[128,8192]{1,0:T(8,128)(2,1)} copy(bf16[128,8192]{1,0:T(8,128)(2,1)} %expert_layer.1) | data formatting | bytes 4194304

commit v3 on v0

v3 whole, which is shorter than its diff:
```python
import functools

import jax
import jax.numpy as jnp
from jax import lax
from jax.experimental import pallas as pl
from jax.experimental.pallas import tpu as pltpu
from jax.sharding import PartitionSpec as P

EPSILON = 1e-05
MESH = pl.DeviceIdType.MESH
SIDE = 4
GROUP = 8
F32 = jnp.float32
BF16 = jnp.bfloat16
NEAR = pl.ds(1, 2)
EXCHANGES = ((0, 512), (512, 512), (1024, 1024), (2048, 2048))
GATHERS = ((0, 0, 512), (0, 512, 512), (0, 1024, 1024), (0, 2048, 2048), (1, 0, 1024), (1, 1024, 1024), (1, 2048, 1024), (1, 3072, 1024))
REDUCES = ((0, 0, 1024), (0, 1024, 1024), (0, 2048, 1024), (0, 3072, 1024), (1, 0, 1024), (1, 1024, 1024), (1, 2048, 1024), (1, 3072, 1024))
RETURNS = ((0, 1024), (1024, 1024), (2048, 1024), (3072, 1024))


def iota(shape, dim):
    return lax.broadcasted_iota(jnp.int32, shape, dim)


def kernel(
    tokens, gain, picks, counts, router, gate, up, down, out,
    tok, w1, w2, so, sr, x, acc, hid, part, r1, f1, red, r2, f2, res, ro, rr, ob, score, mats,
    local_sem, a2a_send, a2a_recv, ag_send, ag_p1, ag_p2, rs_send, rs_p1, rs_p2, ret_send, ret_recv, out_sem,
):
    dp, e = lax.axis_index("dp"), lax.axis_index("expert")
    y, z = dp // SIDE, dp % SIDE
    half = tokens.shape[1] // 2
    ntok = tokens.shape[0]
    hr = x.shape[4]
    rows = 2 * hr
    slots = SIDE * SIDE * hr
    width = gate.shape[2]

    def near(h, axis, step):
        along_y = (h == 0) == (axis == "a")
        if along_y:
            return (lax.rem(y + step + SIDE, SIDE) * SIDE + z, e)
        return (y * SIDE + lax.rem(z + step + SIDE, SIDE), e)

    def other(o):
        return (dp, lax.rem(e + o, GROUP))

    def send(src, dst, ssem, rsem, device):
        pltpu.make_async_remote_copy(
            src_ref=src, dst_ref=dst, send_sem=ssem, recv_sem=rsem, device_id=device, device_id_type=MESH
        ).start()

    def settle(ref, sem):
        pltpu.make_async_copy(ref, ref, sem).wait()

    barrier = pltpu.get_barrier_semaphore()
    for step in (-1, 1):
        for axis in "ab":
            pl.semaphore_signal(barrier, 1, device_id=near(0, axis, step), device_id_type=MESH)
    for o in range(1, GROUP):
        pl.semaphore_signal(barrier, 1, device_id=other(o), device_id_type=MESH)

    loads = []
    for h in range(2):
        cp = pltpu.make_async_copy(tokens.at[:, pl.ds(h * half, half)], tok.at[h], local_sem.at[h])
        cp.start()
        loads.append(cp)
    big = [
        pltpu.make_async_copy(gate.at[0], w1.at[:, pl.ds(0, width)], local_sem.at[2]),
        pltpu.make_async_copy(up.at[0], w1.at[:, pl.ds(width, width)], local_sem.at[3]),
        pltpu.make_async_copy(down.at[0], w2, local_sem.at[4]),
    ]

    nslot = GROUP * 16
    lane = iota((8, nslot), 1)
    lane_e, lane_h, lane_k = lane >> 4, (lane >> 3) & 1, lane & 7
    sub = iota((8, nslot), 0)
    pk = picks[:, 0, :] - (dp * GROUP + e) * ntok
    spread = jnp.zeros((8, nslot), jnp.int32)
    for k in range(8):
        spread = spread + jnp.where(lane_k == k, pk[:, k : k + 1], 0)
    pick_row = jnp.sum(jnp.where(sub == lane_e, spread, 0).astype(F32), axis=0, keepdims=True)
    cnt = jnp.sum(jnp.where(sub == e, counts[...], 0).astype(F32), axis=0, keepdims=True)
    cnt16 = jnp.broadcast_to(cnt, (16, nslot)).astype(BF16)
    src = iota((nslot, nslot), 0) - dp * GROUP
    dst_e = iota((nslot, nslot), 1) >> 4
    same = (src == dst_e).astype(F32).astype(BF16)
    before = ((src >= 0) & (src < dst_e)).astype(F32).astype(BF16)
    cnt_r = jnp.dot(cnt16, same, preferred_element_type=F32)[0:1]
    off_r = jnp.dot(cnt16, before, preferred_element_type=F32)[0:1]
    k_r = lane_k[0:1].astype(F32)
    pos_r = jnp.where(k_r < cnt_r, off_r + k_r, -1.0)

    def placing(n, shift):
        q = iota((2 * n, nslot), 0)
        l = iota((2 * n, nslot), 1)
        return ((q >> shift) == ((l >> 3) & 1)), (q & (n - 1)).astype(F32)

    same_half, t_id = placing(ntok, 7)
    put = jnp.where(same_half & (t_id == pick_row), 1.0, 0.0)
    same_half, p_id = placing(rows, 5)
    pack = jnp.where(same_half & (p_id == pos_r), 1.0, 0.0)
    take_m = put.T.astype(BF16)
    mats[0 : 2 * ntok, :] = put.astype(BF16)
    mats[2 * ntok : 2 * ntok + 2 * rows, :] = pack.astype(BF16)
    unpack_m = pack.T.astype(BF16)

    for cp in loads:
        cp.wait()
    total = jnp.zeros((nslot, 128), F32)
    for c in range(0, half, 1024):
        t = tok[:, :, pl.ds(c, 1024)].reshape(2 * ntok, 1024)
        g = jnp.dot(take_m, t, preferred_element_type=F32)
        so[:, :, pl.ds(c, 1024)] = g.astype(BF16).reshape(GROUP, 16, 1024)
        sq = g * g
        for i in range(1024 // 128):
            total = total + sq[:, i * 128 : (i + 1) * 128]
    ss = jnp.broadcast_to(jnp.sum(total, axis=1, keepdims=True), (nslot, 128))
    h_col = (iota((nslot, 128), 0) >> 3) & 1
    pair = jnp.where(h_col == 0, pltpu.roll(ss, nslot - 8, 0), pltpu.roll(ss, 8, 0))
    inv = lax.rsqrt((ss + pair)[:, 0:1] / (2 * half) + EPSILON)
    first = h_col[:, 0:1] == 0
    text = iota((nslot, 1), 0) < nslot // 2

    def norm(i):
        c, w = EXCHANGES[i]
        at = pl.ds(c, w)
        ga = gain[:, at]
        gb = gain[:, pl.ds(half + c, w)]
        gm = jnp.where(
            first,
            jnp.where(text, ga[0:1], ga[1:2]),
            jnp.where(text, gb[0:1], gb[1:2]),
        )
        g = so[:, :, at].reshape(nslot, w).astype(F32)
        so[:, :, at] = (g * inv * gm).astype(BF16).reshape(GROUP, 16, w)
        if i == 0:
            pl.semaphore_wait(barrier, 4 + GROUP - 1)
        for o in (4, 3, 5, 2, 6, 7, 1):
            to = lax.rem(e + o, GROUP)
            send(so.at[to, :, at], sr.at[e, :, at], a2a_send.at[i], a2a_recv.at[i], other(o))
        sr[e, :, at] = so[e, :, at]

    def load_weights():
        for cp in big:
            cp.start()

    def clear():
        score[...] = jnp.zeros_like(score)

    def packing(i):
        c, w = EXCHANGES[i]
        at = pl.ds(c, w)
        settle(sr.at[pl.ds(0, GROUP - 1), :, at], a2a_recv.at[i])
        packed = jnp.dot(
            mats[2 * ntok : 2 * ntok + 2 * rows, :], sr[:, :, at].reshape(nslot, w), preferred_element_type=F32
        )
        both = packed.astype(BF16)
        for h in range(2):
            for g in range(2):
                x[h, g, 0, 0, :, at] = both[h * rows + g * hr : h * rows + (g + 1) * hr]
        prod = packed[0:rows] * router[:, at].astype(F32)
        prod += packed[rows : 2 * rows] * router[:, pl.ds(half + c, w)].astype(F32)
        s = score[...]
        for t in range(w // 128):
            s = s + prod[:, t * 128 : (t + 1) * 128]
        score[...] = s

    def blk(h, g, da, db, c, w):
        if h == 1:
            da, db = db, da
        return x.at[h, g, da, db, :, pl.ds(c, w)]

    SETS = (0, NEAR, 3)

    def second(i, n):
        g, c, w = GATHERS[i]
        da = SETS[n]
        for h in range(2):
            s = ag_send.at[h, i, 1]
            send(blk(h, g, da, 0, c, w), blk(h, g, da, 1, c, w), s, ag_p2.at[h, i, n, 0], near(h, "b", 1))
            send(blk(h, g, da, 0, c, w), blk(h, g, da, 2, c, w), s, ag_p2.at[h, i, n, 1], near(h, "b", -1))

    def own(i):
        g, c, w = GATHERS[i]
        for h in range(2):
            s = ag_send.at[h, i, 0]
            send(blk(h, g, 0, 0, c, w), blk(h, g, 1, 0, c, w), s, ag_p1.at[h, i, 0], near(h, "a", 1))
            send(blk(h, g, 0, 0, c, w), blk(h, g, 2, 0, c, w), s, ag_p1.at[h, i, 1], near(h, "a", -1))

    def own2(i):
        second(i, 0)

    def first_hop(i):
        g, c, w = GATHERS[i]
        hw = w // 2
        for h in range(2):
            s = ag_send.at[h, i, 0]
            settle(blk(h, g, 1, 0, c, w), ag_p1.at[h, i, 0])
            send(blk(h, g, 1, 0, c, hw), blk(h, g, 3, 0, c, hw), s, ag_p1.at[h, i, 2], near(h, "a", 1))
            settle(blk(h, g, 2, 0, c, w), ag_p1.at[h, i, 1])
            send(blk(h, g, 2, 0, c + hw, hw), blk(h, g, 3, 0, c + hw, hw), s, ag_p1.at[h, i, 3], near(h, "a", -1))
        second(i, 1)

    def second_hop(i):
        g, c, w = GATHERS[i]
        hw = w // 2
        for h in range(2):
            settle(blk(h, g, 3, 0, c, hw), ag_p1.at[h, i, 2])
            settle(blk(h, g, 3, 0, c + hw, hw), ag_p1.at[h, i, 3])
        second(i, 2)

    def forward(i, n):
        g, c, w = GATHERS[i]
        hw = w // 2
        da = SETS[n]
        for h in range(2):
            s = ag_send.at[h, i, 1]
            settle(blk(h, g, da, 1, c, w), ag_p2.at[h, i, n, 0])
            send(blk(h, g, da, 1, c, hw), blk(h, g, da, 3, c, hw), s, ag_p2.at[h, i, n, 2], near(h, "b", 1))
            settle(blk(h, g, da, 2, c, w), ag_p2.at[h, i, n, 1])
            send(blk(h, g, da, 2, c + hw, hw), blk(h, g, da, 3, c + hw, hw), s, ag_p2.at[h, i, n, 3], near(h, "b", -1))

    def gathered(i):
        g, c, w = GATHERS[i]
        hw = w // 2
        if i == 0:
            big[0].wait()
            big[1].wait()
        for h in range(2):
            for n in range(3):
                settle(blk(h, g, SETS[n], 3, c, hw), ag_p2.at[h, i, n, 2])
                settle(blk(h, g, SETS[n], 3, c + hw, hw), ag_p2.at[h, i, n, 3])
        for h in range(2):
            v = jnp.dot(
                x[h, g, :, :, :, pl.ds(c, w)].reshape(slots, w),
                w1[pl.ds(h * half + c, w), :],
                preferred_element_type=F32,
            )
            if c == 0 and h == 0:
                acc[g] = v
            else:
                acc[g] += v

    def hide(g):
        gv, uv = acc[g, :, 0:width], acc[g, :, width : 2 * width]
        hid[g] = (gv / (1.0 + jnp.exp(-gv)) * uv).astype(BF16)
        if g == 0:
            big[2].wait()

    def add(ref, index, more):
        ref[index] = (ref[index].astype(F32) + more.astype(F32)).astype(BF16)

    def multiply(i):
        g, c, w = REDUCES[i]
        hw = w // 2
        lo, hi = pl.ds(c, hw), pl.ds(c + hw, hw)
        for h in range(2):
            for t in range(c, c + w, 256):
                v = jnp.dot(hid[g], w2[:, pl.ds(h * half + t, 256)], preferred_element_type=F32)
                v = v.astype(BF16).reshape(SIDE, SIDE, hr, 256)
                if h == 1:
                    part[h, g, :, :, :, pl.ds(t, 256)] = v
                else:
                    for da in range(SIDE):
                        for db in range(SIDE):
                            part[h, g, db, da, :, pl.ds(t, 256)] = v[da, db]
            s = rs_send.at[h, i, 0]
            send(part.at[h, g, 3, :, :, lo], r1.at[h, g, :, :, lo], s, rs_p1.at[h, i, 0], near(h, "b", -1))
            send(part.at[h, g, 3, :, :, hi], r1.at[h, g, :, :, hi], s, rs_p1.at[h, i, 1], near(h, "b", 1))
            send(part.at[h, g, 1, :, :, hi], f1.at[h, g, 0, :, :, hi], s, rs_p1.at[h, i, 2], near(h, "b", -1))
            send(part.at[h, g, 2, :, :, lo], f1.at[h, g, 1, :, :, lo], s, rs_p1.at[h, i, 3], near(h, "b", 1))

    def first_on(i):
        g, c, w = REDUCES[i]
        hw = w // 2
        lo, hi = pl.ds(c, hw), pl.ds(c + hw, hw)
        for h in range(2):
            s = rs_send.at[h, i, 0]
            settle(r1.at[h, g, :, :, lo], rs_p1.at[h, i, 0])
            add(part, (h, g, 1, slice(None), slice(None), lo), r1[h, g, :, :, lo])
            send(part.at[h, g, 1, :, :, lo], f1.at[h, g, 0, :, :, lo], s, rs_p1.at[h, i, 4], near(h, "b", -1))
            settle(r1.at[h, g, :, :, hi], rs_p1.at[h, i, 1])
            add(part, (h, g, 2, slice(None), slice(None), hi), r1[h, g, :, :, hi])
            send(part.at[h, g, 2, :, :, hi], f1.at[h, g, 1, :, :, hi], s, rs_p1.at[h, i, 5], near(h, "b", 1))

    def first_end(i):
        g, c, w = REDUCES[i]
        hw = w // 2
        at, lo, hi = pl.ds(c, w), pl.ds(c, hw), pl.ds(c + hw, hw)
        for h in range(2):
            settle(f1.at[h, g, 0, :, :, hi], rs_p1.at[h, i, 2])
            settle(f1.at[h, g, 1, :, :, lo], rs_p1.at[h, i, 3])
            settle(f1.at[h, g, 0, :, :, lo], rs_p1.at[h, i, 4])
            settle(f1.at[h, g, 1, :, :, hi], rs_p1.at[h, i, 5])
            red[h, g, :, :, at] = (
                part[h, g, 0, :, :, at].astype(F32)
                + f1[h, g, 0, :, :, at].astype(F32)
                + f1[h, g, 1, :, :, at].astype(F32)
            ).astype(BF16)
            s = rs_send.at[h, i, 1]
            send(red.at[h, g, 3, :, lo], r2.at[h, g, :, lo], s, rs_p2.at[h, i, 0], near(h, "a", -1))
            send(red.at[h, g, 3, :, hi], r2.at[h, g, :, hi], s, rs_p2.at[h, i, 1], near(h, "a", 1))
            send(red.at[h, g, 1, :, hi], f2.at[h, g, 0, :, hi], s, rs_p2.at[h, i, 2], near(h, "a", -1))
            send(red.at[h, g, 2, :, lo], f2.at[h, g, 1, :, lo], s, rs_p2.at[h, i, 3], near(h, "a", 1))

    def second_on(i):
        g, c, w = REDUCES[i]
        hw = w // 2
        lo, hi = pl.ds(c, hw), pl.ds(c + hw, hw)
        for h in range(2):
            s = rs_send.at[h, i, 1]
            settle(r2.at[h, g, :, lo], rs_p2.at[h, i, 0])
            add(red, (h, g, 1, slice(None), lo), r2[h, g, :, lo])
            send(red.at[h, g, 1, :, lo], f2.at[h, g, 0, :, lo], s, rs_p2.at[h, i, 4], near(h, "a", -1))
            settle(r2.at[h, g, :, hi], rs_p2.at[h, i, 1])
            add(red, (h, g, 2, slice(None), hi), r2[h, g, :, hi])
            send(red.at[h, g, 2, :, hi], f2.at[h, g, 1, :, hi], s, rs_p2.at[h, i, 5], near(h, "a", 1))

    def second_end(i):
        g, c, w = REDUCES[i]
        hw = w // 2
        at, lo, hi = pl.ds(c, w), pl.ds(c, hw), pl.ds(c + hw, hw)
        weight = jax.nn.sigmoid(jnp.sum(score[g * hr : (g + 1) * hr, :], axis=1, keepdims=True))
        for h in range(2):
            settle(f2.at[h, g, 0, :, hi], rs_p2.at[h, i, 2])
            settle(f2.at[h, g, 1, :, lo], rs_p2.at[h, i, 3])
            settle(f2.at[h, g, 0, :, lo], rs_p2.at[h, i, 4])
            settle(f2.at[h, g, 1, :, hi], rs_p2.at[h, i, 5])
            v = red[h, g, 0, :, at].astype(F32) + f2[h, g, 0, :, at].astype(F32) + f2[h, g, 1, :, at].astype(F32)
            res[h, g * hr : (g + 1) * hr, at] = (v * weight).astype(BF16)

    def give_back(i):
        c, w = RETURNS[i]
        at = pl.ds(c, w)
        both = jnp.concatenate([res[0, :, at], res[1, :, at]], axis=0)
        back = jnp.dot(unpack_m, both, preferred_element_type=F32)
        ro[:, :, at] = back.astype(BF16).reshape(GROUP, 16, w)
        for o in (4, 3, 5, 2, 6, 7, 1):
            to = lax.rem(e + o, GROUP)
            send(ro.at[to, :, at], rr.at[e, :, at], ret_send.at[i], ret_recv.at[i], other(o))
        rr[e, :, at] = ro[e, :, at]

    def out_copy(i, h):
        c, w = RETURNS[i]
        return pltpu.make_async_copy(
            ob.at[h, :, pl.ds(c, w)], out.at[:, pl.ds(h * half + c, w)], out_sem.at[h, i]
        )

    def finish(i):
        c, w = RETURNS[i]
        at = pl.ds(c, w)
        settle(rr.at[pl.ds(0, GROUP - 1), :, at], ret_recv.at[i])
        v = jnp.dot(mats[0 : 2 * ntok, :], rr[:, :, at].reshape(nslot, w), preferred_element_type=F32)
        t = tok[:, :, at].reshape(2 * ntok, w).astype(F32)
        ob[:, :, at] = (t + v).astype(BF16).reshape(2, ntok, w)
        for h in range(2):
            out_copy(i, h).start()

    norm(0)
    norm(1)
    load_weights()
    norm(2)
    clear()
    packing(0)
    own(0)
    own2(0)
    packing(1)
    own(4)
    own(1)
    norm(3)
    own2(1)
    own2(4)
    first_hop(0)
    packing(2)
    own(5)
    forward(0, 0)
    own(2)
    own2(2)
    forward(1, 0)
    first_hop(1)
    first_hop(4)
    first_hop(2)
    packing(3)
    own(7)
    own(3)
    forward(2, 0)
    own(6)
    second_hop(0)
    first_hop(5)
    second_hop(2)
    first_hop(3)
    second_hop(1)
    forward(0, 2)
    first_hop(6)
    second_hop(4)
    first_hop(7)
    forward(0, 1)
    own2(3)
    forward(1, 2)
    forward(1, 1)
    forward(2, 2)
    second_hop(6)
    forward(4, 0)
    own2(6)
    gathered(0)
    own2(7)
    second_hop(3)
    gathered(1)
    forward(2, 1)
    forward(3, 1)
    own2(5)
    second_hop(5)
    second_hop(7)
    forward(3, 0)
    forward(3, 2)
    forward(7, 1)
    forward(4, 1)
    forward(6, 0)
    gathered(2)
    forward(5, 0)
    forward(7, 0)
    forward(5, 2)
    forward(4, 2)
    forward(6, 1)
    forward(6, 2)
    forward(5, 1)
    forward(7, 2)
    gathered(3)
    hide(0)
    multiply(2)
    gathered(4)
    multiply(1)
    gathered(5)
    gathered(6)
    multiply(0)
    first_on(1)
    gathered(7)
    multiply(3)
    first_on(0)
    hide(1)
    multiply(4)
    multiply(5)
    first_on(2)
    first_on(4)
    first_on(5)
    multiply(6)
    first_end(4)
    first_end(0)
    first_end(5)
    first_on(6)
    first_end(1)
    multiply(7)
    second_on(4)
    second_on(0)
    second_on(5)
    first_end(2)
    first_on(3)
    first_on(7)
    second_end(4)
    second_end(0)
    second_on(1)
    first_end(6)
    give_back(0)
    first_end(3)
    second_on(2)
    second_end(5)
    first_end(7)
    second_end(1)
    second_on(6)
    give_back(1)
    second_end(2)
    second_on(3)
    second_on(7)
    second_end(6)
    give_back(2)
    second_end(3)
    second_end(7)
    give_back(3)
    finish(1)
    finish(0)
    finish(2)
    finish(3)

    for i, (g, c, w) in enumerate(GATHERS):
        for h in range(2):
            settle(x.at[h, g, 0, pl.ds(0, 3), :, pl.ds(c, w)], ag_send.at[h, i, 0])
            settle(x.at[h, g, pl.ds(0, 3), :, :, pl.ds(c, w)], ag_send.at[h, i, 1])
    for i, (g, c, w) in enumerate(REDUCES):
        for h in range(2):
            settle(part.at[h, g, pl.ds(0, 3), :, :, pl.ds(c, w)], rs_send.at[h, i, 0])
            settle(red.at[h, g, pl.ds(0, 3), :, pl.ds(c, w)], rs_send.at[h, i, 1])
    for i, (c, w) in enumerate(EXCHANGES):
        settle(so.at[pl.ds(0, GROUP - 1), :, pl.ds(c, w)], a2a_send.at[i])
    for i, (c, w) in enumerate(RETURNS):
        settle(ro.at[pl.ds(0, GROUP - 1), :, pl.ds(c, w)], ret_send.at[i])
        for h in range(2):
            out_copy(i, h).wait()


def shards(tokens, modality, norm_gain, picks, counts, router, gate_weight, up_weight, down_weight):
    ntok, d = tokens.shape
    half = d // 2
    hidden = gate_weight.shape[2]
    rows = GROUP * picks.shape[2] // 2
    hr = rows // 2
    vmem = pl.BlockSpec(memory_space=pltpu.VMEM)
    anywhere = pl.BlockSpec(memory_space=pl.ANY)
    dma = pltpu.SemaphoreType.DMA
    slots = hr * SIDE * SIDE
    ne, ng, nr, nb = len(EXCHANGES), len(GATHERS), len(REDUCES), len(RETURNS)
    return pl.pallas_call(
        kernel,
        name="expert_layer",
        out_shape=jax.ShapeDtypeStruct((ntok, d), BF16),
        in_specs=[anywhere, vmem, vmem, vmem, vmem, anywhere, anywhere, anywhere],
        out_specs=anywhere,
        scratch_shapes=[
            pltpu.VMEM((2, ntok, half), BF16),
            pltpu.VMEM((d, 2 * hidden), BF16),
            pltpu.VMEM((hidden, d), BF16),
            pltpu.VMEM((GROUP, 16, half), BF16),
            pltpu.VMEM((GROUP, 16, half), BF16),
            pltpu.VMEM((2, 2, SIDE, SIDE, hr, half), BF16),
            pltpu.VMEM((2, slots, 2 * hidden), F32),
            pltpu.VMEM((2, slots, hidden), BF16),
            pltpu.VMEM((2, 2, SIDE, SIDE, hr, half), BF16),
            pltpu.VMEM((2, 2, SIDE, hr, half), BF16),
            pltpu.VMEM((2, 2, 2, SIDE, hr, half), BF16),
            pltpu.VMEM((2, 2, SIDE, hr, half), BF16),
            pltpu.VMEM((2, 2, hr, half), BF16),
            pltpu.VMEM((2, 2, 2, hr, half), BF16),
            pltpu.VMEM((2, rows, half), BF16),
            pltpu.VMEM((GROUP, 16, half), BF16),
            pltpu.VMEM((GROUP, 16, half), BF16),
            pltpu.VMEM((2, ntok, half), BF16),
            pltpu.VMEM((rows, 128), F32),
            pltpu.VMEM((2 * ntok + 2 * rows, GROUP * 16), BF16),
            dma((5,)),
            dma((ne,)),
            dma((ne,)),
            dma((2, ng, 2)),
            dma((2, ng, 4)),
            dma((2, ng, 3, 4)),
            dma((2, nr, 2)),
            dma((2, nr, 6)),
            dma((2, nr, 6)),
            dma((nb,)),
            dma((nb,)),
            dma((2, nb)),
        ],
        compiler_params=pltpu.CompilerParams(
            collective_id=0, has_side_effects=True, vmem_limit_bytes=60 * 2**20
        ),
        cost_estimate=pl.CostEstimate(
            flops=12 * slots * d * hidden, bytes_accessed=16 * 2**20, transcendentals=2 * slots * hidden
        ),
    )(tokens, norm_gain, picks, counts, router, gate_weight, up_weight, down_weight)


def solution(mesh):
    placed = (
        P(("dp", "expert"), None),
        P(("dp", "expert")),
        P(),
        P(None, ("dp", "expert"), None),
        P(),
        P("expert", None),
        P("expert", None, "dp"),
        P("expert", None, "dp"),
        P("expert", "dp", None),
    )
    return jax.shard_map(
        shards, mesh=mesh, in_specs=placed, out_specs=P(("dp", "expert"), None), check_vma=False
    )
```

time: 320 us -> 118 us (0.37)
  waiting for transfers between devices: 237 us -> 0 us
  Pallas kernels: 0 us -> 115 us
  matrix products: 34.3 us -> 0 us
  blocking collectives: 20.8 us -> 0 us
  between operations: 13.5 us -> 0.01 us
  other arithmetic: 6 us -> 0 us
  starting transfers between devices: 5.44 us -> 0 us
    pallas_call x0 -> x1, Pallas kernels: none -> 115 us  [shards(): pl.pallas_call(kernel, name='expert_layer', out_shape=jax.ShapeDtypeStruc...]
    all_gather x1 -> x0, waiting for transfers between devices: 112 us -> none  [expert_block(): piece = lax.all_gather(chosen, 'dp', axis=0, tiled=True)]
    reduce_scatter x1 -> x0, waiting for transfers between devices: 110 us -> none  [expert_block(): lax.psum_scatter((weight[:, None] * jnp.dot(hidden_hidden, down_weight[0]...]
    dot_general x5 -> x0, matrix products: 34.3 us -> none  [the longest x1 10.6 us: expert_block(): jnp.dot(hidden_hidden, down_weight[0], preferred_element_type=jnp.float32)]
    all_to_all x1 -> x0, blocking collectives: 20.8 us -> none  [shards(): lax.all_to_all(outgoing, 'expert', split_axis=0, concat_axis=0, tiled=True)]
    all_to_all x1 -> x0, waiting for transfers between devices: 14.7 us -> none  [shards(): lax.all_to_all(answers.reshape(groups, pick_slots, -1), 'expert', split_a...]
    all_to_all x1 -> x0, starting transfers between devices: 5.21 us -> none  [shards(): lax.all_to_all(answers.reshape(groups, pick_slots, -1), 'expert', split_a...]
  transfers between devices with their start and end apart: 3 -> 0, of which waited for: 3 -> 0; matrix products, arithmetic and copies ran while one was open for 0% -> 0% of each run, Pallas kernels for 0% -> 0%
where the time goes in v3:
time: 118 us
  Pallas kernels  115 us (97%)
  local copies, waits for them, and re-layouts  3.1 us (3%)
    pallas_call x1, Pallas kernels, shards(): pl.pallas_call(kernel, name='expert_layer', out_shape=jax.ShapeDtypeStruc...  115 us
    unnamed x1, local copies, waits for them, and re-layouts  3.1 us

profile of v3, /device:TPU:1, one launch (start us, length us, event | category | flops | bytes accessed | tf_op | source)
XLA Modules:
  0.0 117.7 jit_solution(14850433886986115329)
XLA Ops:
  0.0 114.6 %expert_layer.1 = bf16[128,8192]{1,0:T(8,128)(2,1)} custom-call(bf16[128,8192]{1,0:T(8,128)(2,1)} %tokens.1, f32[2,8192]{1,0:T(2,128)} %gain.1, s32[8,1,8]{2,1,0:T(1,128)} %picks.1, s32[8,128]{1,0:T(8,128)} %counts.1, bf16[1,8192]{1,0:T(2,128)(2,1)} %router.1, bf16[1,8192,256]{2,1,0:T(8,128)(2,1)} %gate.1, bf16[1,8192,256]{2,1,0:T(8,128)(2,1)} %up.1, ...), custom_call_target="tpu_custom_call" | custom-call | flops 6442450944 | bytes 16777216 | tf_op jit(solution)/shard_map/expert_layer/pallas_call | solution.py:514
  114.6 3.1 %copy.10 = bf16[128,8192]{1,0:T(8,128)(2,1)} copy(bf16[128,8192]{1,0:T(8,128)(2,1)} %expert_layer.1) | data formatting | bytes 4194304

commit v4 on v3

--- a/solution.py
+++ b/solution.py
@@ -25,9 +25,9 @@
 
 
 def kernel(
-    tokens, gain, picks, counts, router, gate, up, down, out,
-    tok, w1, w2, so, sr, x, acc, hid, part, r1, f1, red, r2, f2, res, ro, rr, ob, score, mats,
-    local_sem, a2a_send, a2a_recv, ag_send, ag_p1, ag_p2, rs_send, rs_p1, rs_p2, ret_send, ret_recv, out_sem,
+    tokens, gain_in, picks_in, counts_in, router_in, gate, up, down, out,
+    gain, picks, counts, router, tok, w1, w2, so, sr, x, acc, hid, part, r1, f1, red, r2, f2, res, ro, rr, ob, score, mats,
+    local_sem, a2a_send, a2a_recv, ag_send, ag_p1, ag_p2, ag_end, rs_send, rs_p1, rs_p2, ret_send, ret_recv, out_sem,
 ):
     dp, e = lax.axis_index("dp"), lax.axis_index("expert")
     y, z = dp // SIDE, dp % SIDE
@@ -62,21 +62,25 @@
     for o in range(1, GROUP):
         pl.semaphore_signal(barrier, 1, device_id=other(o), device_id_type=MESH)
 
-    loads = []
     for h in range(2):
-        cp = pltpu.make_async_copy(tokens.at[:, pl.ds(h * half, half)], tok.at[h], local_sem.at[h])
+        pltpu.make_async_copy(tokens.at[:, pl.ds(h * half, half)], tok.at[h], local_sem.at[0]).start()
+    small = []
+    for i, (src, dst) in enumerate(((picks_in, picks), (counts_in, counts), (gain_in, gain), (router_in, router))):
+        cp = pltpu.make_async_copy(src, dst, local_sem.at[3 + i])
         cp.start()
-        loads.append(cp)
+        small.append(cp)
     big = [
-        pltpu.make_async_copy(gate.at[0], w1.at[:, pl.ds(0, width)], local_sem.at[2]),
-        pltpu.make_async_copy(up.at[0], w1.at[:, pl.ds(width, width)], local_sem.at[3]),
-        pltpu.make_async_copy(down.at[0], w2, local_sem.at[4]),
+        pltpu.make_async_copy(gate.at[0], w1.at[:, pl.ds(0, width)], local_sem.at[1]),
+        pltpu.make_async_copy(up.at[0], w1.at[:, pl.ds(width, width)], local_sem.at[1]),
+        pltpu.make_async_copy(down.at[0], w2, local_sem.at[2]),
     ]
 
     nslot = GROUP * 16
     lane = iota((8, nslot), 1)
     lane_e, lane_h, lane_k = lane >> 4, (lane >> 3) & 1, lane & 7
     sub = iota((8, nslot), 0)
+    small[0].wait()
+    small[1].wait()
     pk = picks[:, 0, :] - (dp * GROUP + e) * ntok
     spread = jnp.zeros((8, nslot), jnp.int32)
     for k in range(8):
@@ -107,7 +111,8 @@
     mats[2 * ntok : 2 * ntok + 2 * rows, :] = pack.astype(BF16)
     unpack_m = pack.T.astype(BF16)
 
-    for cp in loads:
+    settle(tok, local_sem.at[0])
+    for cp in small[2:]:
         cp.wait()
     total = jnp.zeros((nslot, 128), F32)
     for c in range(0, half, 1024):
@@ -140,7 +145,7 @@
             pl.semaphore_wait(barrier, 4 + GROUP - 1)
         for o in (4, 3, 5, 2, 6, 7, 1):
             to = lax.rem(e + o, GROUP)
-            send(so.at[to, :, at], sr.at[e, :, at], a2a_send.at[i], a2a_recv.at[i], other(o))
+            send(so.at[to, :, at], sr.at[e, :, at], a2a_send.at[0], a2a_recv.at[i], other(o))
         sr[e, :, at] = so[e, :, at]
 
     def load_weights():
@@ -178,17 +183,17 @@
     def second(i, n):
         g, c, w = GATHERS[i]
         da = SETS[n]
-        for h in range(2):
-            s = ag_send.at[h, i, 1]
-            send(blk(h, g, da, 0, c, w), blk(h, g, da, 1, c, w), s, ag_p2.at[h, i, n, 0], near(h, "b", 1))
-            send(blk(h, g, da, 0, c, w), blk(h, g, da, 2, c, w), s, ag_p2.at[h, i, n, 1], near(h, "b", -1))
+        s, r = ag_send.at[1], ag_p2.at[i, n]
+        for h in range(2):
+            send(blk(h, g, da, 0, c, w), blk(h, g, da, 1, c, w), s, r, near(h, "b", 1))
+            send(blk(h, g, da, 0, c, w), blk(h, g, da, 2, c, w), s, r, near(h, "b", -1))
 
     def own(i):
         g, c, w = GATHERS[i]
-        for h in range(2):
-            s = ag_send.at[h, i, 0]
-            send(blk(h, g, 0, 0, c, w), blk(h, g, 1, 0, c, w), s, ag_p1.at[h, i, 0], near(h, "a", 1))
-            send(blk(h, g, 0, 0, c, w), blk(h, g, 2, 0, c, w), s, ag_p1.at[h, i, 1], near(h, "a", -1))
+        s, r = ag_send.at[0], ag_p1.at[i, 0]
+        for h in range(2):
+            send(blk(h, g, 0, 0, c, w), blk(h, g, 1, 0, c, w), s, r, near(h, "a", 1))
+            send(blk(h, g, 0, 0, c, w), blk(h, g, 2, 0, c, w), s, r, near(h, "a", -1))
 
     def own2(i):
         second(i, 0)
@@ -196,43 +201,33 @@
     def first_hop(i):
         g, c, w = GATHERS[i]
         hw = w // 2
-        for h in range(2):
-            s = ag_send.at[h, i, 0]
-            settle(blk(h, g, 1, 0, c, w), ag_p1.at[h, i, 0])
-            send(blk(h, g, 1, 0, c, hw), blk(h, g, 3, 0, c, hw), s, ag_p1.at[h, i, 2], near(h, "a", 1))
-            settle(blk(h, g, 2, 0, c, w), ag_p1.at[h, i, 1])
-            send(blk(h, g, 2, 0, c + hw, hw), blk(h, g, 3, 0, c + hw, hw), s, ag_p1.at[h, i, 3], near(h, "a", -1))
+        s, r = ag_send.at[0], ag_p1.at[i, 1]
+        settle(x.at[0, g, 0, :, :, pl.ds(c, w)], ag_p1.at[i, 0])
+        for h in range(2):
+            send(blk(h, g, 1, 0, c, hw), blk(h, g, 3, 0, c, hw), s, r, near(h, "a", 1))
+            send(blk(h, g, 2, 0, c + hw, hw), blk(h, g, 3, 0, c + hw, hw), s, r, near(h, "a", -1))
         second(i, 1)
 
     def second_hop(i):
         g, c, w = GATHERS[i]
-        hw = w // 2
-        for h in range(2):
-            settle(blk(h, g, 3, 0, c, hw), ag_p1.at[h, i, 2])
-            settle(blk(h, g, 3, 0, c + hw, hw), ag_p1.at[h, i, 3])
+        settle(x.at[0, g, 0, pl.ds(0, 2), :, pl.ds(c, w)], ag_p1.at[i, 1])
         second(i, 2)
 
     def forward(i, n):
         g, c, w = GATHERS[i]
         hw = w // 2
         da = SETS[n]
-        for h in range(2):
-            s = ag_send.at[h, i, 1]
-            settle(blk(h, g, da, 1, c, w), ag_p2.at[h, i, n, 0])
-            send(blk(h, g, da, 1, c, hw), blk(h, g, da, 3, c, hw), s, ag_p2.at[h, i, n, 2], near(h, "b", 1))
-            settle(blk(h, g, da, 2, c, w), ag_p2.at[h, i, n, 1])
-            send(blk(h, g, da, 2, c + hw, hw), blk(h, g, da, 3, c + hw, hw), s, ag_p2.at[h, i, n, 3], near(h, "b", -1))
+        s, r = ag_send.at[1], ag_end.at[i]
+        settle(x.at[0, g, pl.ds(0, 2 if n == 1 else 1), :, :, pl.ds(c, w)], ag_p2.at[i, n])
+        for h in range(2):
+            send(blk(h, g, da, 1, c, hw), blk(h, g, da, 3, c, hw), s, r, near(h, "b", 1))
+            send(blk(h, g, da, 2, c + hw, hw), blk(h, g, da, 3, c + hw, hw), s, r, near(h, "b", -1))
 
     def gathered(i):
         g, c, w = GATHERS[i]
-        hw = w // 2
         if i == 0:
-            big[0].wait()
-            big[1].wait()
-        for h in range(2):
-            for n in range(3):
-                settle(blk(h, g, SETS[n], 3, c, hw), ag_p2.at[h, i, n, 2])
-                settle(blk(h, g, SETS[n], 3, c + hw, hw), ag_p2.at[h, i, n, 3])
+            settle(w1, local_sem.at[1])
+        settle(x.at[0, g, pl.ds(0, 2), :, :, pl.ds(c, w)], ag_end.at[i])
         for h in range(2):
             v = jnp.dot(
                 x[h, g, :, :, :, pl.ds(c, w)].reshape(slots, w),
@@ -248,7 +243,7 @@
         gv, uv = acc[g, :, 0:width], acc[g, :, width : 2 * width]
         hid[g] = (gv / (1.0 + jnp.exp(-gv)) * uv).astype(BF16)
         if g == 0:
-            big[2].wait()
+            settle(w2, local_sem.at[2])
 
     def add(ref, index, more):
         ref[index] = (ref[index].astype(F32) + more.astype(F32)).astype(BF16)
@@ -267,68 +262,60 @@
                     for da in range(SIDE):
                         for db in range(SIDE):
                             part[h, g, db, da, :, pl.ds(t, 256)] = v[da, db]
-            s = rs_send.at[h, i, 0]
-            send(part.at[h, g, 3, :, :, lo], r1.at[h, g, :, :, lo], s, rs_p1.at[h, i, 0], near(h, "b", -1))
-            send(part.at[h, g, 3, :, :, hi], r1.at[h, g, :, :, hi], s, rs_p1.at[h, i, 1], near(h, "b", 1))
-            send(part.at[h, g, 1, :, :, hi], f1.at[h, g, 0, :, :, hi], s, rs_p1.at[h, i, 2], near(h, "b", -1))
-            send(part.at[h, g, 2, :, :, lo], f1.at[h, g, 1, :, :, lo], s, rs_p1.at[h, i, 3], near(h, "b", 1))
+            s = rs_send.at[0]
+            send(part.at[h, g, 3, :, :, lo], r1.at[h, g, :, :, lo], s, rs_p1.at[i, 0], near(h, "b", -1))
+            send(part.at[h, g, 3, :, :, hi], r1.at[h, g, :, :, hi], s, rs_p1.at[i, 0], near(h, "b", 1))
+            send(part.at[h, g, 1, :, :, hi], f1.at[h, g, 0, :, :, hi], s, rs_p1.at[i, 1], near(h, "b", -1))
+            send(part.at[h, g, 2, :, :, lo], f1.at[h, g, 1, :, :, lo], s, rs_p1.at[i, 1], near(h, "b", 1))
 
     def first_on(i):
         g, c, w = REDUCES[i]
         hw = w // 2
         lo, hi = pl.ds(c, hw), pl.ds(c + hw, hw)
-        for h in range(2):
-            s = rs_send.at[h, i, 0]
-            settle(r1.at[h, g, :, :, lo], rs_p1.at[h, i, 0])
+        s = rs_send.at[0]
+        settle(r1.at[:, g, :, :, pl.ds(c, w)], rs_p1.at[i, 0])
+        for h in range(2):
             add(part, (h, g, 1, slice(None), slice(None), lo), r1[h, g, :, :, lo])
-            send(part.at[h, g, 1, :, :, lo], f1.at[h, g, 0, :, :, lo], s, rs_p1.at[h, i, 4], near(h, "b", -1))
-            settle(r1.at[h, g, :, :, hi], rs_p1.at[h, i, 1])
+            send(part.at[h, g, 1, :, :, lo], f1.at[h, g, 0, :, :, lo], s, rs_p1.at[i, 1], near(h, "b", -1))
             add(part, (h, g, 2, slice(None), slice(None), hi), r1[h, g, :, :, hi])
-            send(part.at[h, g, 2, :, :, hi], f1.at[h, g, 1, :, :, hi], s, rs_p1.at[h, i, 5], near(h, "b", 1))
+            send(part.at[h, g, 2, :, :, hi], f1.at[h, g, 1, :, :, hi], s, rs_p1.at[i, 1], near(h, "b", 1))
 
     def first_end(i):
         g, c, w = REDUCES[i]
         hw = w // 2
         at, lo, hi = pl.ds(c, w), pl.ds(c, hw), pl.ds(c + hw, hw)
-        for h in range(2):
-            settle(f1.at[h, g, 0, :, :, hi], rs_p1.at[h, i, 2])
-            settle(f1.at[h, g, 1, :, :, lo], rs_p1.at[h, i, 3])
-            settle(f1.at[h, g, 0, :, :, lo], rs_p1.at[h, i, 4])
-            settle(f1.at[h, g, 1, :, :, hi], rs_p1.at[h, i, 5])
+        settle(f1.at[:, g, :, :, :, at], rs_p1.at[i, 1])
+        for h in range(2):
             red[h, g, :, :, at] = (
                 part[h, g, 0, :, :, at].astype(F32)
                 + f1[h, g, 0, :, :, at].astype(F32)
                 + f1[h, g, 1, :, :, at].astype(F32)
             ).astype(BF16)
-            s = rs_send.at[h, i, 1]
-            send(red.at[h, g, 3, :, lo], r2.at[h, g, :, lo], s, rs_p2.at[h, i, 0], near(h, "a", -1))
-            send(red.at[h, g, 3, :, hi], r2.at[h, g, :, hi], s, rs_p2.at[h, i, 1], near(h, "a", 1))
-            send(red.at[h, g, 1, :, hi], f2.at[h, g, 0, :, hi], s, rs_p2.at[h, i, 2], near(h, "a", -1))
-            send(red.at[h, g, 2, :, lo], f2.at[h, g, 1, :, lo], s, rs_p2.at[h, i, 3], near(h, "a", 1))
+            s = rs_send.at[1]
+            send(red.at[h, g, 3, :, lo], r2.at[h, g, :, lo], s, rs_p2.at[i, 0], near(h, "a", -1))
+            send(red.at[h, g, 3, :, hi], r2.at[h, g, :, hi], s, rs_p2.at[i, 0], near(h, "a", 1))
+            send(red.at[h, g, 1, :, hi], f2.at[h, g, 0, :, hi], s, rs_p2.at[i, 1], near(h, "a", -1))
+            send(red.at[h, g, 2, :, lo], f2.at[h, g, 1, :, lo], s, rs_p2.at[i, 1], near(h, "a", 1))
 
     def second_on(i):
         g, c, w = REDUCES[i]
         hw = w // 2
         lo, hi = pl.ds(c, hw), pl.ds(c + hw, hw)
-        for h in range(2):
-            s = rs_send.at[h, i, 1]
-            settle(r2.at[h, g, :, lo], rs_p2.at[h, i, 0])
+        s = rs_send.at[1]
+        settle(r2.at[:, g, :, pl.ds(c, w)], rs_p2.at[i, 0])
+        for h in range(2):
             add(red, (h, g, 1, slice(None), lo), r2[h, g, :, lo])
-            send(red.at[h, g, 1, :, lo], f2.at[h, g, 0, :, lo], s, rs_p2.at[h, i, 4], near(h, "a", -1))
-            settle(r2.at[h, g, :, hi], rs_p2.at[h, i, 1])
+            send(red.at[h, g, 1, :, lo], f2.at[h, g, 0, :, lo], s, rs_p2.at[i, 1], near(h, "a", -1))
             add(red, (h, g, 2, slice(None), hi), r2[h, g, :, hi])
-            send(red.at[h, g, 2, :, hi], f2.at[h, g, 1, :, hi], s, rs_p2.at[h, i, 5], near(h, "a", 1))
+            send(red.at[h, g, 2, :, hi], f2.at[h, g, 1, :, hi], s, rs_p2.at[i, 1], near(h, "a", 1))
 
     def second_end(i):
         g, c, w = REDUCES[i]
         hw = w // 2
         at, lo, hi = pl.ds(c, w), pl.ds(c, hw), pl.ds(c + hw, hw)
         weight = jax.nn.sigmoid(jnp.sum(score[g * hr : (g + 1) * hr, :], axis=1, keepdims=True))
-        for h in range(2):
-            settle(f2.at[h, g, 0, :, hi], rs_p2.at[h, i, 2])
-            settle(f2.at[h, g, 1, :, lo], rs_p2.at[h, i, 3])
-            settle(f2.at[h, g, 0, :, lo], rs_p2.at[h, i, 4])
-            settle(f2.at[h, g, 1, :, hi], rs_p2.at[h, i, 5])
+        settle(f2.at[:, g, :, :, at], rs_p2.at[i, 1])
+        for h in range(2):
             v = red[h, g, 0, :, at].astype(F32) + f2[h, g, 0, :, at].astype(F32) + f2[h, g, 1, :, at].astype(F32)
             res[h, g * hr : (g + 1) * hr, at] = (v * weight).astype(BF16)
 
@@ -340,13 +327,13 @@
         ro[:, :, at] = back.astype(BF16).reshape(GROUP, 16, w)
         for o in (4, 3, 5, 2, 6, 7, 1):
             to = lax.rem(e + o, GROUP)
-            send(ro.at[to, :, at], rr.at[e, :, at], ret_send.at[i], ret_recv.at[i], other(o))
+            send(ro.at[to, :, at], rr.at[e, :, at], ret_send.at[0], ret_recv.at[i], other(o))
         rr[e, :, at] = ro[e, :, at]
 
     def out_copy(i, h):
         c, w = RETURNS[i]
         return pltpu.make_async_copy(
-            ob.at[h, :, pl.ds(c, w)], out.at[:, pl.ds(h * half + c, w)], out_sem.at[h, i]
+            ob.at[h, :, pl.ds(c, w)], out.at[:, pl.ds(h * half + c, w)], out_sem.at[0]
         )
 
     def finish(i):
@@ -484,20 +471,13 @@
     finish(2)
     finish(3)
 
-    for i, (g, c, w) in enumerate(GATHERS):
-        for h in range(2):
-            settle(x.at[h, g, 0, pl.ds(0, 3), :, pl.ds(c, w)], ag_send.at[h, i, 0])
-            settle(x.at[h, g, pl.ds(0, 3), :, :, pl.ds(c, w)], ag_send.at[h, i, 1])
-    for i, (g, c, w) in enumerate(REDUCES):
-        for h in range(2):
-            settle(part.at[h, g, pl.ds(0, 3), :, :, pl.ds(c, w)], rs_send.at[h, i, 0])
-            settle(red.at[h, g, pl.ds(0, 3), :, pl.ds(c, w)], rs_send.at[h, i, 1])
-    for i, (c, w) in enumerate(EXCHANGES):
-        settle(so.at[pl.ds(0, GROUP - 1), :, pl.ds(c, w)], a2a_send.at[i])
-    for i, (c, w) in enumerate(RETURNS):
-        settle(ro.at[pl.ds(0, GROUP - 1), :, pl.ds(c, w)], ret_send.at[i])
-        for h in range(2):
-            out_copy(i, h).wait()
+    settle(x.at[:, :, 0, pl.ds(0, 3)], ag_send.at[0])
+    settle(x.at[:, :, pl.ds(0, 3)], ag_send.at[1])
+    settle(part.at[:, :, pl.ds(0, 3)], rs_send.at[0])
+    settle(red.at[:, :, pl.ds(0, 3)], rs_send.at[1])
+    settle(so.at[pl.ds(0, GROUP - 1)], a2a_send.at[0])
+    settle(ro.at[pl.ds(0, GROUP - 1)], ret_send.at[0])
+    settle(ob, out_sem.at[0])
 
 
 def shards(tokens, modality, norm_gain, picks, counts, router, gate_weight, up_weight, down_weight):
@@ -506,7 +486,6 @@
     hidden = gate_weight.shape[2]
     rows = GROUP * picks.shape[2] // 2
     hr = rows // 2
-    vmem = pl.BlockSpec(memory_space=pltpu.VMEM)
     anywhere = pl.BlockSpec(memory_space=pl.ANY)
     dma = pltpu.SemaphoreType.DMA
     slots = hr * SIDE * SIDE
@@ -515,9 +494,13 @@
         kernel,
         name="expert_layer",
         out_shape=jax.ShapeDtypeStruct((ntok, d), BF16),
-        in_specs=[anywhere, vmem, vmem, vmem, vmem, anywhere, anywhere, anywhere],
+        in_specs=[anywhere] * 8,
         out_specs=anywhere,
         scratch_shapes=[
+            pltpu.VMEM(norm_gain.shape, F32),
+            pltpu.VMEM(picks.shape, jnp.int32),
+            pltpu.VMEM(counts.shape, jnp.int32),
+            pltpu.VMEM(router.shape, BF16),
             pltpu.VMEM((2, ntok, half), BF16),
             pltpu.VMEM((d, 2 * hidden), BF16),
             pltpu.VMEM((hidden, d), BF16),
@@ -538,18 +521,19 @@
             pltpu.VMEM((2, ntok, half), BF16),
             pltpu.VMEM((rows, 128), F32),
             pltpu.VMEM((2 * ntok + 2 * rows, GROUP * 16), BF16),
-            dma((5,)),
+            dma((7,)),
+            dma((1,)),
             dma((ne,)),
-            dma((ne,)),
-            dma((2, ng, 2)),
-            dma((2, ng, 4)),
-            dma((2, ng, 3, 4)),
-            dma((2, nr, 2)),
-            dma((2, nr, 6)),
-            dma((2, nr, 6)),
+            dma((2,)),
+            dma((ng, 2)),
+            dma((ng, 3)),
+            dma((ng,)),
+            dma((2,)),
+            dma((nr, 2)),
+            dma((nr, 2)),
+            dma((1,)),
             dma((nb,)),
-            dma((nb,)),
-            dma((2, nb)),
+            dma((1,)),
         ],
         compiler_params=pltpu.CompilerParams(
             collective_id=0, has_side_effects=True, vmem_limit_bytes=60 * 2**20

time: 118 us -> 113 us (0.958)
  Pallas kernels: 115 us -> 110 us
    pallas_call x1, Pallas kernels: 115 us -> 110 us  [shards(): pl.pallas_call(kernel, name='expert_layer', out_shape=jax.ShapeDtypeStruc...]
where the time goes in v4:
time: 113 us
  Pallas kernels  110 us (97%)
  local copies, waits for them, and re-layouts  3.1 us (3%)
    pallas_call x1, Pallas kernels, shards(): pl.pallas_call(kernel, name='expert_layer', out_shape=jax.ShapeDtypeStruc...  110 us
    unnamed x1, local copies, waits for them, and re-layouts  3.1 us

profile of v4, /device:TPU:1, one launch (start us, length us, event | category | flops | bytes accessed | tf_op | source)
XLA Modules:
  0.0 113.3 jit_solution(1258100924149449129)
XLA Ops:
  0.0 110.2 %expert_layer.1 = bf16[128,8192]{1,0:T(8,128)(2,1)} custom-call(bf16[128,8192]{1,0:T(8,128)(2,1)} %tokens.1, f32[2,8192]{1,0:T(2,128)} %gain_in.1, s32[8,1,8]{2,1,0:T(1,128)} %picks_in.1, s32[8,128]{1,0:T(8,128)} %counts_in.1, bf16[1,8192]{1,0:T(2,128)(2,1)} %router_in.1, bf16[1,8192,256]{2,1,0:T(8,128)(2,1)} %gate.1, bf16[1,8192,256]{2,1,0:T(8,128)(2,1)} %up.1, ...), custom_call_target="tpu_custom_call" | custom-call | flops 6442450944 | bytes 16777216 | tf_op jit(solution)/shard_map/expert_layer/pallas_call | solution.py:493
  110.2 3.1 %copy.10 = bf16[128,8192]{1,0:T(8,128)(2,1)} copy(bf16[128,8192]{1,0:T(8,128)(2,1)} %expert_layer.1) | data formatting | bytes 4194304

commit v5 on v4

--- a/solution.py
+++ b/solution.py
@@ -11,13 +11,14 @@
 MESH = pl.DeviceIdType.MESH
 SIDE = 4
 GROUP = 8
+PIECES = 2
 F32 = jnp.float32
 BF16 = jnp.bfloat16
 NEAR = pl.ds(1, 2)
 EXCHANGES = ((0, 512), (512, 512), (1024, 1024), (2048, 2048))
-GATHERS = ((0, 0, 512), (0, 512, 512), (0, 1024, 1024), (0, 2048, 2048), (1, 0, 1024), (1, 1024, 1024), (1, 2048, 1024), (1, 3072, 1024))
-REDUCES = ((0, 0, 1024), (0, 1024, 1024), (0, 2048, 1024), (0, 3072, 1024), (1, 0, 1024), (1, 1024, 1024), (1, 2048, 1024), (1, 3072, 1024))
-RETURNS = ((0, 1024), (1024, 1024), (2048, 1024), (3072, 1024))
+GATHERS = ((0, 0, 512), (0, 512, 512), (0, 1024, 1024), (0, 2048, 1024), (0, 3072, 1024), (1, 0, 1024), (1, 1024, 1024), (1, 2048, 1024), (1, 3072, 1024))
+REDUCES = ((0, 0, 1024), (0, 1024, 1024), (0, 2048, 1024), (0, 3072, 1024), (1, 0, 768), (1, 768, 768), (1, 1536, 768), (1, 2304, 768), (1, 3072, 512), (1, 3584, 512))
+RETURNS = ((0, 768), (768, 768), (1536, 768), (2304, 768), (3072, 512), (3584, 512))
 
 
 def iota(shape, dim):
@@ -25,9 +26,9 @@
 
 
 def kernel(
-    tokens, gain_in, picks_in, counts_in, router_in, gate, up, down, out,
-    gain, picks, counts, router, tok, w1, w2, so, sr, x, acc, hid, part, r1, f1, red, r2, f2, res, ro, rr, ob, score, mats,
-    local_sem, a2a_send, a2a_recv, ag_send, ag_p1, ag_p2, ag_end, rs_send, rs_p1, rs_p2, ret_send, ret_recv, out_sem,
+    tokens, gain_in, picks_in, counts_in, router_in, gate, up, down, rr, put_out,
+    gain, picks, counts, router, tok, w1, w2, so, sr, x, acc, hid, part, r1, f1, red, r2, f2, res, ro, score, mats,
+    local_sem, a2a_send, a2a_recv, ag_send, ag_p1, ag_p2, ag_end, rs_send, rs_p1, rs_p2, ret_send, ret_recv,
 ):
     dp, e = lax.axis_index("dp"), lax.axis_index("expert")
     y, z = dp // SIDE, dp % SIDE
@@ -109,6 +110,8 @@
     take_m = put.T.astype(BF16)
     mats[0 : 2 * ntok, :] = put.astype(BF16)
     mats[2 * ntok : 2 * ntok + 2 * rows, :] = pack.astype(BF16)
+    put_copy = pltpu.make_async_copy(mats.at[pl.ds(0, 2 * ntok)], put_out, local_sem.at[7])
+    put_copy.start()
     unpack_m = pack.T.astype(BF16)
 
     settle(tok, local_sem.at[0])
@@ -328,148 +331,158 @@
         for o in (4, 3, 5, 2, 6, 7, 1):
             to = lax.rem(e + o, GROUP)
             send(ro.at[to, :, at], rr.at[e, :, at], ret_send.at[0], ret_recv.at[i], other(o))
-        rr[e, :, at] = ro[e, :, at]
-
-    def out_copy(i, h):
-        c, w = RETURNS[i]
-        return pltpu.make_async_copy(
-            ob.at[h, :, pl.ds(c, w)], out.at[:, pl.ds(h * half + c, w)], out_sem.at[0]
-        )
+        pltpu.make_async_copy(ro.at[e, :, at], rr.at[e, :, at], local_sem.at[8]).start()
 
     def finish(i):
         c, w = RETURNS[i]
-        at = pl.ds(c, w)
-        settle(rr.at[pl.ds(0, GROUP - 1), :, at], ret_recv.at[i])
-        v = jnp.dot(mats[0 : 2 * ntok, :], rr[:, :, at].reshape(nslot, w), preferred_element_type=F32)
-        t = tok[:, :, at].reshape(2 * ntok, w).astype(F32)
-        ob[:, :, at] = (t + v).astype(BF16).reshape(2, ntok, w)
-        for h in range(2):
-            out_copy(i, h).start()
+        settle(rr.at[pl.ds(0, GROUP - 1), :, pl.ds(c, w)], ret_recv.at[i])
 
     norm(0)
+    load_weights()
     norm(1)
-    load_weights()
     norm(2)
     clear()
     packing(0)
     own(0)
     own2(0)
     packing(1)
-    own(4)
+    own(5)
     own(1)
     norm(3)
+    own2(5)
     own2(1)
-    own2(4)
     first_hop(0)
     packing(2)
-    own(5)
-    forward(0, 0)
     own(2)
-    own2(2)
+    own(6)
+    first_hop(5)
     forward(1, 0)
     first_hop(1)
-    first_hop(4)
+    forward(0, 0)
     first_hop(2)
     packing(3)
+    own(4)
     own(7)
+    forward(0, 1)
+    forward(5, 0)
+    own2(3)
     own(3)
+    forward(1, 1)
+    own2(4)
+    second_hop(2)
+    own2(7)
+    first_hop(4)
+    own2(2)
+    second_hop(0)
+    own(8)
+    second_hop(1)
+    first_hop(3)
+    second_hop(4)
+    forward(2, 1)
     forward(2, 0)
-    own(6)
-    second_hop(0)
-    first_hop(5)
-    second_hop(2)
-    first_hop(3)
-    second_hop(1)
+    second_hop(5)
+    forward(3, 0)
     forward(0, 2)
+    forward(2, 2)
+    forward(5, 1)
+    second_hop(3)
+    forward(7, 0)
     first_hop(6)
-    second_hop(4)
+    forward(1, 2)
     first_hop(7)
-    forward(0, 1)
-    own2(3)
-    forward(1, 2)
-    forward(1, 1)
-    forward(2, 2)
+    forward(3, 2)
+    first_hop(8)
+    own2(6)
+    forward(3, 1)
+    forward(4, 1)
+    forward(4, 2)
+    own2(8)
+    forward(4, 0)
+    forward(6, 1)
     second_hop(6)
-    forward(4, 0)
-    own2(6)
+    forward(8, 1)
     gathered(0)
-    own2(7)
-    second_hop(3)
     gathered(1)
-    forward(2, 1)
-    forward(3, 1)
-    own2(5)
-    second_hop(5)
+    second_hop(8)
     second_hop(7)
-    forward(3, 0)
-    forward(3, 2)
+    forward(5, 2)
     forward(7, 1)
-    forward(4, 1)
+    gathered(2)
+    gathered(3)
     forward(6, 0)
-    gathered(2)
-    forward(5, 0)
-    forward(7, 0)
-    forward(5, 2)
-    forward(4, 2)
-    forward(6, 1)
+    gathered(4)
+    forward(8, 0)
+    hide(0)
+    multiply(0)
+    multiply(1)
+    forward(7, 2)
+    forward(8, 2)
     forward(6, 2)
-    forward(5, 1)
-    forward(7, 2)
-    gathered(3)
-    hide(0)
+    first_on(0)
+    multiply(3)
+    gathered(5)
     multiply(2)
-    gathered(4)
-    multiply(1)
-    gathered(5)
     gathered(6)
-    multiply(0)
+    gathered(7)
+    gathered(8)
     first_on(1)
-    gathered(7)
-    multiply(3)
-    first_on(0)
     hide(1)
     multiply(4)
     multiply(5)
+    multiply(6)
+    first_on(4)
+    first_end(1)
+    multiply(8)
+    first_end(0)
+    first_on(5)
+    multiply(7)
+    first_end(4)
+    first_on(6)
     first_on(2)
-    first_on(4)
-    first_on(5)
-    multiply(6)
-    first_end(4)
-    first_end(0)
+    multiply(9)
     first_end(5)
-    first_on(6)
-    first_end(1)
-    multiply(7)
+    first_on(7)
+    first_end(6)
+    first_on(8)
     second_on(4)
     second_on(0)
-    second_on(5)
     first_end(2)
     first_on(3)
-    first_on(7)
+    second_on(5)
+    second_on(1)
+    first_end(7)
+    first_on(9)
     second_end(4)
     second_end(0)
-    second_on(1)
-    first_end(6)
+    first_end(8)
+    second_on(6)
+    second_on(2)
     give_back(0)
     first_end(3)
-    second_on(2)
     second_end(5)
-    first_end(7)
     second_end(1)
-    second_on(6)
     give_back(1)
+    second_on(7)
+    first_end(9)
+    second_on(8)
+    second_end(6)
     second_end(2)
+    give_back(2)
     second_on(3)
-    second_on(7)
-    second_end(6)
-    give_back(2)
-    second_end(3)
     second_end(7)
     give_back(3)
+    second_on(9)
+    second_end(8)
+    second_end(3)
+    give_back(4)
     finish(1)
+    second_end(9)
+    give_back(5)
+    finish(2)
     finish(0)
-    finish(2)
     finish(3)
+    finish(4)
+    finish(5)
 
     settle(x.at[:, :, 0, pl.ds(0, 3)], ag_send.at[0])
     settle(x.at[:, :, pl.ds(0, 3)], ag_send.at[1])
@@ -477,7 +490,39 @@
     settle(red.at[:, :, pl.ds(0, 3)], rs_send.at[1])
     settle(so.at[pl.ds(0, GROUP - 1)], a2a_send.at[0])
     settle(ro.at[pl.ds(0, GROUP - 1)], ret_send.at[0])
-    settle(ob, out_sem.at[0])
+    settle(ro.at[0], local_sem.at[8])
+    put_copy.wait()
+
+
+def add_returned(tokens, returned, put_in, out, tok, back, put, ob, load_sem, store_sem, put_sem):
+    ntok, half = tokens.shape[0], tokens.shape[1] // 2
+    w = half // PIECES
+    put_copy = pltpu.make_async_copy(put_in, put, put_sem.at[0])
+    put_copy.start()
+    loads, stores = [], []
+    for i in range(PIECES):
+        at = pl.ds(i * w, w)
+        row = [pltpu.make_async_copy(returned.at[:, :, at], back.at[:, :, at], load_sem.at[i, 2])]
+        for h in range(2):
+            there = pl.ds(h * half + i * w, w)
+            row.append(pltpu.make_async_copy(tokens.at[:, there], tok.at[h, :, at], load_sem.at[i, h]))
+        for cp in row:
+            cp.start()
+        loads.append(row)
+    put_copy.wait()
+    for i in range(PIECES):
+        at = pl.ds(i * w, w)
+        for cp in loads[i]:
+            cp.wait()
+        v = jnp.dot(put[...], back[:, :, at].reshape(GROUP * 16, w), preferred_element_type=F32)
+        t = tok[:, :, at].reshape(2 * ntok, w).astype(F32)
+        ob[:, :, at] = (t + v).astype(BF16).reshape(2, ntok, w)
+        for h in range(2):
+            cp = pltpu.make_async_copy(ob.at[h, :, at], out.at[:, pl.ds(h * half + i * w, w)], store_sem.at[i, h])
+            cp.start()
+            stores.append(cp)
+    for cp in stores:
+        cp.wait()
 
 
 def shards(tokens, modality, norm_gain, picks, counts, router, gate_weight, up_weight, down_weight):
@@ -490,12 +535,15 @@
     dma = pltpu.SemaphoreType.DMA
     slots = hr * SIDE * SIDE
     ne, ng, nr, nb = len(EXCHANGES), len(GATHERS), len(REDUCES), len(RETURNS)
-    return pl.pallas_call(
+    returned, put = pl.pallas_call(
         kernel,
         name="expert_layer",
-        out_shape=jax.ShapeDtypeStruct((ntok, d), BF16),
+        out_shape=(
+            jax.ShapeDtypeStruct((GROUP, 16, half), BF16),
+            jax.ShapeDtypeStruct((2 * ntok, GROUP * 16), BF16),
+        ),
         in_specs=[anywhere] * 8,
-        out_specs=anywhere,
+        out_specs=(anywhere, anywhere),
         scratch_shapes=[
             pltpu.VMEM(norm_gain.shape, F32),
             pltpu.VMEM(picks.shape, jnp.int32),
@@ -517,11 +565,9 @@
             pltpu.VMEM((2, 2, 2, hr, half), BF16),
             pltpu.VMEM((2, rows, half), BF16),
             pltpu.VMEM((GROUP, 16, half), BF16),
-            pltpu.VMEM((GROUP, 16, half), BF16),
-            pltpu.VMEM((2, ntok, half), BF16),
             pltpu.VMEM((rows, 128), F32),
             pltpu.VMEM((2 * ntok + 2 * rows, GROUP * 16), BF16),
-            dma((7,)),
+            dma((9,)),
             dma((1,)),
             dma((ne,)),
             dma((2,)),
@@ -533,15 +579,34 @@
             dma((nr, 2)),
             dma((1,)),
             dma((nb,)),
-            dma((1,)),
         ],
         compiler_params=pltpu.CompilerParams(
-            collective_id=0, has_side_effects=True, vmem_limit_bytes=60 * 2**20
+            collective_id=0, has_side_effects=True, vmem_limit_bytes=56 * 2**20
         ),
         cost_estimate=pl.CostEstimate(
             flops=12 * slots * d * hidden, bytes_accessed=16 * 2**20, transcendentals=2 * slots * hidden
         ),
     )(tokens, norm_gain, picks, counts, router, gate_weight, up_weight, down_weight)
+    return pl.pallas_call(
+        add_returned,
+        name="add_returned",
+        out_shape=jax.ShapeDtypeStruct((ntok, d), BF16),
+        in_specs=[anywhere] * 3,
+        out_specs=anywhere,
+        scratch_shapes=[
+            pltpu.VMEM((2, ntok, half), BF16),
+            pltpu.VMEM((GROUP, 16, half), BF16),
+            pltpu.VMEM((2 * ntok, GROUP * 16), BF16),
+            pltpu.VMEM((2, ntok, half), BF16),
+            dma((PIECES, 3)),
+            dma((PIECES, 2)),
+            dma((1,)),
+        ],
+        compiler_params=pltpu.CompilerParams(vmem_limit_bytes=57 * 2**20),
+        cost_estimate=pl.CostEstimate(
+            flops=4 * ntok * GROUP * 16 * half, bytes_accessed=5 * ntok * d, transcendentals=0
+        ),
+    )(tokens, returned, put)
 
 
 def solution(mesh):

time: 113 us -> 112 us (level)
  local copies, waits for them, and re-layouts: 3.1 us -> 0 us
  Pallas kernels: 110 us -> 112 us
    unnamed x1 -> x0, local copies, waits for them, and re-layouts: 3.1 us -> none
    pallas_call x1 -> x2, Pallas kernels: 110 us -> 112 us  [the longest x1 109 us: shards(): pl.pallas_call(kernel, name='expert_layer', out_shape=(jax.ShapeDtypeStru...]
where the time goes in v5:
time: 112 us
  Pallas kernels  112 us (100%)
    pallas_call x1, Pallas kernels, shards(): pl.pallas_call(kernel, name='expert_layer', out_shape=(jax.ShapeDtypeStru...  109 us
    pallas_call x1, Pallas kernels, shards(): pl.pallas_call(add_returned, name='add_returned', out_shape=jax.ShapeDtyp...  3.55 us

profile of v5, /device:TPU:1, one launch (start us, length us, event | category | flops | bytes accessed | tf_op | source)
XLA Modules:
  0.0 112.3 jit_solution(565936763097894791)
XLA Ops:
  0.0 108.6 %expert_layer.1 = (bf16[8,16,4096]{2,1,0:T(8,128)(2,1)}, bf16[256,128]{1,0:T(8,128)(2,1)}) custom-call(bf16[128,8192]{1,0:T(8,128)(2,1)} %tokens.3, f32[2,8192]{1,0:T(2,128)} %gain_in.1, s32[8,1,8]{2,1,0:T(1,128)} %picks_in.1, s32[8,128]{1,0:T(8,128)} %counts_in.1, bf16[1,8192]{1,0:T(2,128)(2,1)} %router_in.1, bf16[1,8192,256]{2,1,0:T(8,128)(2,1)} %gate.1, ...), custom_call_target="tpu_custom_call" | custom-call | flops 6442450944 | bytes 16777216 | tf_op jit(solution)/shard_map/expert_layer/pallas_call | solution.py:538
  108.6 3.5 %add_returned.1 = bf16[128,8192]{1,0:T(8,128)(2,1)} custom-call(bf16[128,8192]{1,0:T(8,128)(2,1)} %tokens.3, bf16[8,16,4096]{2,1,0:T(8,128)(2,1)} %get-tuple-element.7.returned, bf16[256,128]{1,0:T(8,128)(2,1)} %get-tuple-element.8.put_in), custom_call_target="tpu_custom_call" | custom-call | flops 268435456 | bytes 5242880 | tf_op jit(solution)/shard_map/add_returned/pallas_call | solution.py:590

commit v6 on v5

--- a/solution.py
+++ b/solution.py
@@ -16,9 +16,9 @@
 BF16 = jnp.bfloat16
 NEAR = pl.ds(1, 2)
 EXCHANGES = ((0, 512), (512, 512), (1024, 1024), (2048, 2048))
-GATHERS = ((0, 0, 512), (0, 512, 512), (0, 1024, 1024), (0, 2048, 1024), (0, 3072, 1024), (1, 0, 1024), (1, 1024, 1024), (1, 2048, 1024), (1, 3072, 1024))
-REDUCES = ((0, 0, 1024), (0, 1024, 1024), (0, 2048, 1024), (0, 3072, 1024), (1, 0, 768), (1, 768, 768), (1, 1536, 768), (1, 2304, 768), (1, 3072, 512), (1, 3584, 512))
-RETURNS = ((0, 768), (768, 768), (1536, 768), (2304, 768), (3072, 512), (3584, 512))
+GATHERS = ((0, 0, 512), (0, 512, 512), (0, 1024, 1024), (0, 2048, 2048), (1, 0, 1024), (1, 1024, 1024), (1, 2048, 1024), (1, 3072, 1024))
+REDUCES = ((0, 0, 1024), (0, 1024, 1024), (0, 2048, 1024), (0, 3072, 1024), (1, 0, 1024), (1, 1024, 1024), (1, 2048, 1024), (1, 3072, 1024))
+RETURNS = ((0, 1024), (1024, 1024), (2048, 1024), (3072, 1024))
 
 
 def iota(shape, dim):
@@ -81,23 +81,11 @@
     lane_e, lane_h, lane_k = lane >> 4, (lane >> 3) & 1, lane & 7
     sub = iota((8, nslot), 0)
     small[0].wait()
-    small[1].wait()
     pk = picks[:, 0, :] - (dp * GROUP + e) * ntok
     spread = jnp.zeros((8, nslot), jnp.int32)
     for k in range(8):
         spread = spread + jnp.where(lane_k == k, pk[:, k : k + 1], 0)
     pick_row = jnp.sum(jnp.where(sub == lane_e, spread, 0).astype(F32), axis=0, keepdims=True)
-    cnt = jnp.sum(jnp.where(sub == e, counts[...], 0).astype(F32), axis=0, keepdims=True)
-    cnt16 = jnp.broadcast_to(cnt, (16, nslot)).astype(BF16)
-    src = iota((nslot, nslot), 0) - dp * GROUP
-    dst_e = iota((nslot, nslot), 1) >> 4
-    same = (src == dst_e).astype(F32).astype(BF16)
-    before = ((src >= 0) & (src < dst_e)).astype(F32).astype(BF16)
-    cnt_r = jnp.dot(cnt16, same, preferred_element_type=F32)[0:1]
-    off_r = jnp.dot(cnt16, before, preferred_element_type=F32)[0:1]
-    k_r = lane_k[0:1].astype(F32)
-    pos_r = jnp.where(k_r < cnt_r, off_r + k_r, -1.0)
-
     def placing(n, shift):
         q = iota((2 * n, nslot), 0)
         l = iota((2 * n, nslot), 1)
@@ -105,14 +93,10 @@
 
     same_half, t_id = placing(ntok, 7)
     put = jnp.where(same_half & (t_id == pick_row), 1.0, 0.0)
-    same_half, p_id = placing(rows, 5)
-    pack = jnp.where(same_half & (p_id == pos_r), 1.0, 0.0)
     take_m = put.T.astype(BF16)
     mats[0 : 2 * ntok, :] = put.astype(BF16)
-    mats[2 * ntok : 2 * ntok + 2 * rows, :] = pack.astype(BF16)
     put_copy = pltpu.make_async_copy(mats.at[pl.ds(0, 2 * ntok)], put_out, local_sem.at[7])
     put_copy.start()
-    unpack_m = pack.T.astype(BF16)
 
     settle(tok, local_sem.at[0])
     for cp in small[2:]:
@@ -151,6 +135,24 @@
             send(so.at[to, :, at], sr.at[e, :, at], a2a_send.at[0], a2a_recv.at[i], other(o))
         sr[e, :, at] = so[e, :, at]
 
+    def pack_matrices():
+        small[1].wait()
+        cnt = jnp.sum(jnp.where(sub == e, counts[...], 0).astype(F32), axis=0, keepdims=True)
+        cnt16 = jnp.broadcast_to(cnt, (16, nslot)).astype(BF16)
+        src = iota((nslot, nslot), 0) - dp * GROUP
+        dst_e = iota((nslot, nslot), 1) >> 4
+        same = (src == dst_e).astype(F32).astype(BF16)
+        before = ((src >= 0) & (src < dst_e)).astype(F32).astype(BF16)
+        cnt_r = jnp.dot(cnt16, same, preferred_element_type=F32)[0:1]
+        off_r = jnp.dot(cnt16, before, preferred_element_type=F32)[0:1]
+        k_r = lane_k[0:1].astype(F32)
+        pos_r = jnp.where(k_r < cnt_r, off_r + k_r, -1.0)
+        same_half, p_id = placing(rows, 5)
+        pack = jnp.where(same_half & (p_id == pos_r), 1.0, 0.0)
+        mats[2 * ntok : 2 * ntok + 2 * rows, :] = pack.astype(BF16)
+        unpack_m = pack.T.astype(BF16)
+        return unpack_m
+
     def load_weights():
         for cp in big:
             cp.start()
@@ -338,6 +340,7 @@
         settle(rr.at[pl.ds(0, GROUP - 1), :, pl.ds(c, w)], ret_recv.at[i])
 
     norm(0)
+    unpack_m = pack_matrices()
     load_weights()
     norm(1)
     norm(2)
@@ -346,143 +349,121 @@
     own(0)
     own2(0)
     packing(1)
-    own(5)
+    own(4)
     own(1)
-    norm(3)
-    own2(5)
+    own2(4)
     own2(1)
     first_hop(0)
+    norm(3)
     packing(2)
     own(2)
+    forward(0, 0)
+    own2(2)
+    own(5)
+    first_hop(4)
+    first_hop(1)
+    second_hop(0)
+    first_hop(2)
+    first_hop(5)
+    forward(2, 0)
+    packing(3)
+    own2(3)
+    forward(1, 1)
+    own(3)
+    second_hop(2)
+    own2(6)
+    second_hop(1)
+    own2(5)
+    own(7)
     own(6)
-    first_hop(5)
-    forward(1, 0)
-    first_hop(1)
-    forward(0, 0)
-    first_hop(2)
-    packing(3)
-    own(4)
-    own(7)
-    forward(0, 1)
-    forward(5, 0)
-    own2(3)
-    own(3)
-    forward(1, 1)
-    own2(4)
-    second_hop(2)
-    own2(7)
-    first_hop(4)
-    own2(2)
-    second_hop(0)
-    own(8)
-    second_hop(1)
-    first_hop(3)
-    second_hop(4)
-    forward(2, 1)
-    forward(2, 0)
-    second_hop(5)
     forward(3, 0)
     forward(0, 2)
+    forward(0, 1)
+    first_hop(3)
     forward(2, 2)
-    forward(5, 1)
+    first_hop(7)
+    forward(1, 2)
+    second_hop(4)
+    forward(1, 0)
+    first_hop(6)
+    own2(7)
     second_hop(3)
+    forward(2, 1)
+    second_hop(7)
+    second_hop(5)
+    forward(5, 0)
+    gathered(0)
+    second_hop(6)
+    forward(3, 1)
+    forward(3, 2)
+    gathered(1)
     forward(7, 0)
-    first_hop(6)
-    forward(1, 2)
-    first_hop(7)
-    forward(3, 2)
-    first_hop(8)
-    own2(6)
-    forward(3, 1)
     forward(4, 1)
-    forward(4, 2)
-    own2(8)
-    forward(4, 0)
-    forward(6, 1)
-    second_hop(6)
-    forward(8, 1)
-    gathered(0)
-    gathered(1)
-    second_hop(8)
-    second_hop(7)
     forward(5, 2)
     forward(7, 1)
+    forward(6, 0)
     gathered(2)
+    forward(6, 1)
+    forward(7, 2)
+    forward(4, 2)
+    forward(6, 2)
+    forward(4, 0)
+    forward(5, 1)
     gathered(3)
-    forward(6, 0)
-    gathered(4)
-    forward(8, 0)
     hide(0)
+    multiply(3)
+    multiply(2)
     multiply(0)
     multiply(1)
-    forward(7, 2)
-    forward(8, 2)
-    forward(6, 2)
-    first_on(0)
-    multiply(3)
+    gathered(4)
     gathered(5)
-    multiply(2)
     gathered(6)
     gathered(7)
-    gathered(8)
-    first_on(1)
     hide(1)
     multiply(4)
     multiply(5)
+    first_on(4)
+    first_on(0)
     multiply(6)
-    first_on(4)
-    first_end(1)
-    multiply(8)
+    first_on(1)
+    first_on(5)
+    first_on(6)
     first_end(0)
-    first_on(5)
+    first_end(4)
     multiply(7)
-    first_end(4)
-    first_on(6)
+    first_end(5)
     first_on(2)
-    multiply(9)
-    first_end(5)
-    first_on(7)
-    first_end(6)
-    first_on(8)
     second_on(4)
     second_on(0)
+    first_on(3)
+    first_end(1)
+    first_on(7)
+    second_on(5)
+    first_end(6)
+    second_end(4)
     first_end(2)
-    first_on(3)
-    second_on(5)
     second_on(1)
+    first_end(3)
+    second_end(0)
+    give_back(0)
     first_end(7)
-    first_on(9)
-    second_end(4)
-    second_end(0)
-    first_end(8)
+    second_end(5)
     second_on(6)
     second_on(2)
-    give_back(0)
-    first_end(3)
-    second_end(5)
     second_end(1)
     give_back(1)
+    second_on(3)
     second_on(7)
-    first_end(9)
-    second_on(8)
     second_end(6)
     second_end(2)
     give_back(2)
-    second_on(3)
+    second_end(3)
     second_end(7)
     give_back(3)
-    second_on(9)
-    second_end(8)
-    second_end(3)
-    give_back(4)
     finish(1)
-    second_end(9)
-    give_back(5)
+    finish(0)
     finish(2)
-    finish(0)
     finish(3)
-    finish(4)
-    finish(5)
 
     settle(x.at[:, :, 0, pl.ds(0, 3)], ag_send.at[0])
     settle(x.at[:, :, pl.ds(0, 3)], ag_send.at[1])

time: 112 us -> 112 us (level)
  no operation moved by 1% of the time
where the time goes in v6:
time: 112 us
  Pallas kernels  112 us (100%)
    pallas_call x1, Pallas kernels, shards(): pl.pallas_call(kernel, name='expert_layer', out_shape=(jax.ShapeDtypeStru...  109 us
    pallas_call x1, Pallas kernels, shards(): pl.pallas_call(add_returned, name='add_returned', out_shape=jax.ShapeDtyp...  3.55 us

profile of v6, /device:TPU:1, one launch (start us, length us, event | category | flops | bytes accessed | tf_op | source)
XLA Modules:
  0.0 112.1 jit_solution(7022154492966772037)
XLA Ops:
  0.0 108.6 %expert_layer.1 = (bf16[8,16,4096]{2,1,0:T(8,128)(2,1)}, bf16[256,128]{1,0:T(8,128)(2,1)}) custom-call(bf16[128,8192]{1,0:T(8,128)(2,1)} %tokens.3, f32[2,8192]{1,0:T(2,128)} %gain_in.1, s32[8,1,8]{2,1,0:T(1,128)} %picks_in.1, s32[8,128]{1,0:T(8,128)} %counts_in.1, bf16[1,8192]{1,0:T(2,128)(2,1)} %router_in.1, bf16[1,8192,256]{2,1,0:T(8,128)(2,1)} %gate.1, ...), custom_call_target="tpu_custom_call" | custom-call | flops 6442450944 | bytes 16777216 | tf_op jit(solution)/shard_map/expert_layer/pallas_call | solution.py:519
  108.6 3.6 %add_returned.1 = bf16[128,8192]{1,0:T(8,128)(2,1)} custom-call(bf16[128,8192]{1,0:T(8,128)(2,1)} %tokens.3, bf16[8,16,4096]{2,1,0:T(8,128)(2,1)} %get-tuple-element.7.returned, bf16[256,128]{1,0:T(8,128)(2,1)} %get-tuple-element.8.put_in), custom_call_target="tpu_custom_call" | custom-call | flops 268435456 | bytes 5242880 | tf_op jit(solution)/shard_map/add_returned/pallas_call | solution.py:571
